TPU v7x, 32 devices: a whole 2x2x4 slice. The times are simulated.
32 devices in a mesh: gx: 8 (over z, y), gy: 4 (over x, core).
Axes of the slice: x: 2, y: 2, z: 4, core: 2. Of those that a mesh axis runs over, the one named last changes fastest.
Arguments:
- positions: float32 [3, 1024], P(None, ('gx', 'gy')), may hold values from -4 to 4
- species: int32 [1024], P(('gx', 'gy')), may hold values from 0 to 7
- atom_count: int32 [32], P(('gx', 'gy')), may hold values from 10 to 32, as said below
- send_list: int32 [32, 8, 4], P(('gx', 'gy')), may hold values from 0 to 31, as said below
- edges: int32 [32, 2, 256], P(('gx', 'gy')), may hold values from 0 to 63, as said below
- centre_embed: float32 [512, 8], replicated, may hold values from -3 to 3
- neighbour_embed: float32 [512, 8], replicated, may hold values from -3 to 3
- radial_weight: float32 [512, 8], replicated, may hold values from -2 to 2
- env_weight: float32 [2, 64, 512], replicated, may hold values from -0.25 to 0.25
- latent_weight: float32 [2, 512, 704], replicated, may hold values from -0.21875 to 0.21875
- out_weight: float32 [512, 512], replicated, may hold values from -0.25 to 0.25
- head_weight: float32 [2, 512], replicated, may hold values from -0.25 to 0.25
Outputs:
- atom_energy: float32 [1024], P(('gx', 'gy'))
- forces: float32 [3, 1024], P(None, ('gx', 'gy'))
Inputs may be any that keep to these rules, and one draw needn't show every extreme that they name: Device p's live atoms are its slots 0 to atom_count[p] - 1, the rest are padding; its live edges are its first 8 atom_count[p] edge slots. send_list[p, k, g] is a live atom of device p; the 4 atoms of one (p, k) are distinct and are sent to the device at offset k. `edges`: row 0 is a live atom slot of the device; row 1 is a live atom slot other than the centre, or a ghost slot 32 + k * 4 + g.
All inputs are finite; a program needn't handle non-finite values.
Results may differ from a plain program's by a relative error of at most 0.00025.
Values sent between devices are 32-bit elements; how exact they have to be, the bound alone decides.
No kernel may reach another device: no remote copies, remote signals or barrier semaphores. Data moves between devices by JAX's collectives and lax.ppermute only.
A program may use at most 64 MiB of HBM per device.

v0:
```python
import math

import jax
import jax.numpy as jnp
from jax import lax
from jax.sharding import PartitionSpec as P

offset_x = (-1, -1, -1, 0, 0, 1, 1, 1)
offset_y = (-1, 0, 1, -1, 1, -1, 0, 1)
highest = lax.Precision.HIGHEST


def extended(value, sides, width):
    for axis, dim in sides:
        peers, length = (lax.axis_size(axis), value.shape[dim])
        up = [(i, (i + 1) % peers) for i in range(peers)]
        down = [(j, i) for i, j in up]
        last = lax.slice_in_dim(value, length - width, length, axis=dim)
        initial = lax.slice_in_dim(value, 0, width, axis=dim)
        before = lax.ppermute(last, axis, up)
        after = lax.ppermute(initial, axis, down)
        value = jnp.concatenate([before, value, after], axis=dim)
    return value


def parity():
    return jnp.array([1.0, -1.0, -1.0, -1.0, 1.0, 1.0, 1.0, 1.0, 1.0], dtype=jnp.float32)


def harmonics(unit):
    root = math.sqrt(3.0)
    along_x, along_y, along_z = (unit[0], unit[1], unit[2])
    return jnp.stack(
        [
            jnp.ones_like(along_x),
            along_x,
            along_y,
            along_z,
            root * along_x * along_y,
            root * along_y * along_z,
            0.5 * (3.0 * along_z * along_z - 1.0),
            root * along_x * along_z,
            0.5 * root * (along_x * along_x - along_y * along_y),
        ]
    )


def geometry(start, finish, count_basis):
    offset = finish - start
    squared = jnp.sum(offset * offset, axis=0)
    unit = offset / jnp.sqrt(1.0 + squared)
    length = jnp.sqrt(squared)
    centres = 0.5 * jnp.arange(count_basis, dtype=jnp.float32)
    basis = jnp.exp(-2.0 * (length[None, :] - centres[:, None]) ** 2)
    return (unit, basis, harmonics(unit))


def refine(hidden, env_centre, env_other, harm, weight):
    sign = parity()[None, :, None]
    product = (env_centre + env_other * sign) * harm[None]
    scalars = jnp.concatenate(
        [hidden, product[:, 0], jnp.sum(product[:, 1:4], axis=1), jnp.sum(product[:, 4:9], axis=1)],
        axis=0,
    )
    return hidden + jax.nn.silu(jnp.dot(weight, scalars, precision=highest))


def to_grid(items):
    padding = jnp.zeros_like(items[:1])
    joined = jnp.concatenate([items[:4], padding, items[4:]], axis=0)
    return joined.reshape((3, 3) + items.shape[1:])


def deliver(items, backward):
    grid = to_grid(items)
    if backward:
        padded = extended(grid, (("gx", 0), ("gy", 1)), 1)
    else:
        padded = extended(grid, (("gx", 0), ("gy", 1)), 1)
    return jnp.stack(
        [padded[2 + 2 * offset_x[direction], 2 + 2 * offset_y[direction]] for direction in range(8)]
    )


def flatten(items):
    return items.transpose(1, 0, 2).reshape(items.shape[1], -1)


def spread(values, sends):
    rows = values.shape[0]
    picked = jnp.take(values, sends, axis=1).reshape(rows, 8, -1).transpose(1, 0, 2)
    ghosts = deliver(picked, False)
    return jnp.concatenate([values, flatten(ghosts)], axis=1)


def collect(partial_value, sends, atoms):
    rows = partial_value.shape[0]
    own = partial_value[:, :atoms]
    ghost_items = partial_value[:, atoms:].reshape(rows, 8, -1).transpose(1, 0, 2)
    returned = deliver(ghost_items, True)
    return own.at[:, sends].add(flatten(returned))


def local(
    positions,
    species,
    atom_count,
    send_list,
    edges,
    centre_embed,
    neighbour_embed,
    radial_weight,
    env_weight,
    latent_weight,
    out_weight,
    head_weight,
):
    atoms = positions.shape[1]
    channels = env_weight.shape[1]
    count_edges = edges.shape[2]
    sends = send_list[0].reshape(-1)
    slots_all = atoms + sends.shape[0]
    centre = edges[0, 0]
    other = edges[0, 1]
    per_atom = count_edges // atoms
    live = (jnp.arange(count_edges, dtype=jnp.int32) < per_atom * atom_count[0]).astype(jnp.float32)
    coords = jnp.concatenate([positions, species.astype(jnp.float32)[None]], axis=0)
    pool = spread(coords, sends)
    start = pool[:, centre]
    finish = pool[:, other]
    unit, basis, harm = geometry(start[:3], finish[:3], radial_weight.shape[1])
    kinds = jnp.arange(centre_embed.shape[1], dtype=jnp.float32)[:, None]
    onehot_centre = (start[3][None, :] == kinds).astype(jnp.float32)
    onehot_other = (finish[3][None, :] == kinds).astype(jnp.float32)
    inner = jnp.dot(radial_weight, basis, precision=highest)
    inner = inner + jnp.dot(centre_embed, onehot_centre, precision=highest)
    inner = inner + jnp.dot(neighbour_embed, onehot_other, precision=highest)
    hidden = jax.nn.silu(inner)
    parity_rows = jnp.tile(parity(), channels)[:, None]
    for layer in range(env_weight.shape[0]):
        weights_e = jnp.dot(env_weight[layer], hidden, precision=highest)
        contrib = (weights_e[:, None, :] * harm[None]).reshape(channels * 9, count_edges) * (
            live * 0.25
        )
        partial_value = jnp.zeros((channels * 9, slots_all), jnp.float32)
        partial_value = (
            partial_value.at[:, centre].add(contrib).at[:, other].add(contrib * parity_rows)
        )
        env_own = collect(partial_value, sends, atoms)
        env_pool = spread(env_own, sends)
        env_centre = env_pool[:, centre].reshape(channels, 9, count_edges)
        env_other = env_pool[:, other].reshape(channels, 9, count_edges)
        hidden = refine(hidden, env_centre, env_other, harm, latent_weight[layer])
    latent = jax.nn.silu(jnp.dot(out_weight, hidden, precision=highest))
    heads = jnp.dot(head_weight, latent, precision=highest)
    energy_e = 0.5 * heads[0] * live
    push = heads[1] * live * unit
    partial_value = jnp.zeros((4, slots_all), jnp.float32)
    partial_value = partial_value.at[:, centre].add(jnp.concatenate([energy_e[None], push], axis=0))
    partial_value = partial_value.at[:, other].add(jnp.concatenate([energy_e[None], -push], axis=0))
    totals = collect(partial_value, sends, atoms)
    return (totals[0], totals[1:4])


def solution(mesh):
    placed = (
        P(None, ("gx", "gy")),
        P(("gx", "gy")),
        P(("gx", "gy")),
        P(("gx", "gy"), None, None),
        P(("gx", "gy"), None, None),
        P(),
        P(),
        P(),
        P(),
        P(),
        P(),
        P(),
    )
    return jax.shard_map(
        local,
        mesh=mesh,
        in_specs=placed,
        out_specs=(P(("gx", "gy")), P(None, ("gx", "gy"))),
        check_vma=False,
    )
```

profile of v0, /device:TPU:0, one launch (start us, length us, event | category | flops | bytes accessed | tf_op | source)
XLA Modules:
  0.0 137.3 jit_solution(4717216159563292602)
XLA Ops:
  5.3 6.1 %collective-permute-start.1 = (f32[1,3,4,4]{3,2,1,0:T(4,128)S(1)}, f32[1,3,4,4]{3,2,1,0:T(4,128)S(1)}, u32[]{:S(2)}, u32[]{:S(2)}) collective-permute-start(f32[1,3,4,4]{3,2,1,0:T(4,128)S(1)} %bitcast.394), channel_id=1, source_target_pairs={{4,0},{8,4},{12,8},{16,12},{20,16},{24,20},{28,24},{0,28},{5,1},{9... | collective-permute-start | bytes 584 | tf_op jit(solution)/shard_map/ppermute | solution.py:21
  12.7 5.0 %collective-permute-done = f32[1,3,4,4]{3,2,1,0:T(4,128)S(1)} collective-permute-done((f32[1,3,4,4]{3,2,1,0:T(4,128)S(1)}, f32[1,3,4,4]{3,2,1,0:T(4,128)S(1)}, u32[]{:S(2)}, u32[]{:S(2)}) %collective-permute-start) | collective-permute-done | bytes 224 | tf_op jit(solution)/shard_map/ppermute | solution.py:20
  18.6 1.8 %collective-permute-start.3 = (f32[5,1,4,4]{3,2,1,0:T(4,128)S(1)}, f32[5,1,4,4]{3,2,1,0:T(4,128)S(1)}, u32[]{:S(2)}, u32[]{:S(2)}) collective-permute-start(f32[5,1,4,4]{3,2,1,0:T(4,128)S(1)} %get-tuple-element.49), channel_id=1, source_target_pairs={{1,0},{2,1},{3,2},{0,3},{5,4},{6,5},{7,6},{4,7},{9,8},{10,9},{11,1... | collective-permute-start | bytes 968 | tf_op jit(solution)/shard_map/ppermute | solution.py:21
  24.5 1.4 %fusion.58 = f32[256,512]{1,0:T(8,128)S(1)} fusion(f32[512,8]{0,1:T(8,128)} %param.24, f32[8]{0:T(128)S(1)} %iota_multiply_fusion, f32[256]{0:T(256)S(1)} %get-tuple-element.71), kind=kOutput, calls=%fused_computation.212 | convolution fusion | flops 12589056 | bytes 541728 | tf_op jit(solution)/shard_map/dot_general | solution.py:135
  30.4 2.3 %scatter_custom_fusion = f32[576,64]{0,1:T(8,128)S(1)} fusion(s32[256]{0:T(256)S(1)} %bitcast.400, f32[256,576]{1,0:T(8,128)S(1)} %copy.135, f32[]{:T(128)} %constant.24.clone.1), kind=kCustom, calls=%fused_computation.144 | custom fusion | flops 147456 | bytes 147460 | tf_op jit(solution)/shard_map/scatter-add | solution.py:147
  32.7 2.3 %scatter_fusion = f32[576,64]{0,1:T(8,128)S(1)} fusion(f32[576,64]{0,1:T(8,128)S(1)} %scatter_custom_fusion, s32[256]{0:T(256)S(1)} %bitcast.387, f32[256,576]{1,0:T(8,128)S(1)} %copy.136), kind=kCustom, calls=%fused_computation.10 | custom fusion | flops 147456 | bytes 1770496 | tf_op jit(solution)/shard_map/scatter-add | solution.py:147
  35.2 4.7 %collective-permute-start.5 = (f32[1,3,576,4]{2,3,1,0:T(4,128)S(1)}, f32[1,3,576,4]{2,3,1,0:T(4,128)S(1)}, u32[]{:S(2)}, u32[]{:S(2)}) collective-permute-start(f32[1,3,576,4]{2,3,1,0:T(4,128)S(1)} %get-tuple-element.42), channel_id=1, source_target_pairs={{4,0},{8,4},{12,8},{16,12},{20,16},{24,20},{28,24},{0,28},{5,1},{9... | collective-permute-start | bytes 82952 | tf_op jit(solution)/shard_map/ppermute | solution.py:21
  40.0 1.8 %collective-permute-done.4 = f32[1,3,576,4]{2,3,1,0:T(4,128)S(1)} collective-permute-done((f32[1,3,576,4]{2,3,1,0:T(4,128)S(1)}, f32[1,3,576,4]{2,3,1,0:T(4,128)S(1)}, u32[]{:S(2)}, u32[]{:S(2)}) %collective-permute-start.4) | collective-permute-done | bytes 27680 | tf_op jit(solution)/shard_map/ppermute | solution.py:20
  42.3 1.3 collective-permute-start.7
  43.6 1.8 %collective-permute-done.6 = f32[5,1,576,4]{2,3,1,0:T(4,128)S(1)} collective-permute-done((f32[5,1,576,4]{2,3,1,0:T(4,128)S(1)}, f32[5,1,576,4]{2,3,1,0:T(4,128)S(1)}, u32[]{:S(2)}, u32[]{:S(2)}) %collective-permute-start.6) | collective-permute-done | bytes 46112 | tf_op jit(solution)/shard_map/ppermute | solution.py:20
  47.2 4.8 %collective-permute-start.9 = (f32[1,3,576,4]{2,3,1,0:T(4,128)S(1)}, f32[1,3,576,4]{2,3,1,0:T(4,128)S(1)}, u32[]{:S(2)}, u32[]{:S(2)}) collective-permute-start(f32[1,3,576,4]{2,3,1,0:T(4,128)S(1)} %get-tuple-element.38), channel_id=1, source_target_pairs={{4,0},{8,4},{12,8},{16,12},{20,16},{24,20},{28,24},{0,28},{5,1},{9... | collective-permute-start | bytes 82952 | tf_op jit(solution)/shard_map/ppermute | solution.py:21
  52.0 1.7 %collective-permute-done.8 = f32[1,3,576,4]{2,3,1,0:T(4,128)S(1)} collective-permute-done((f32[1,3,576,4]{2,3,1,0:T(4,128)S(1)}, f32[1,3,576,4]{2,3,1,0:T(4,128)S(1)}, u32[]{:S(2)}, u32[]{:S(2)}) %collective-permute-start.8) | collective-permute-done | bytes 27680 | tf_op jit(solution)/shard_map/ppermute | solution.py:20
  54.6 1.1 collective-permute-start.11
  55.7 1.7 %collective-permute-done.10 = f32[5,1,576,4]{2,3,1,0:T(4,128)S(1)} collective-permute-done((f32[5,1,576,4]{2,3,1,0:T(4,128)S(1)}, f32[5,1,576,4]{2,3,1,0:T(4,128)S(1)}, u32[]{:S(2)}, u32[]{:S(2)}) %collective-permute-start.10) | collective-permute-done | bytes 46112 | tf_op jit(solution)/shard_map/ppermute | solution.py:20
  57.5 1.1 gather_fusion.4
  58.6 2.0 %gather_fusion.3 = f32[256,576]{1,0:T(8,128)} fusion(f32[576,64]{0,1:T(8,128)S(1)} %constant_dynamic-update-slice_fusion.24, s32[1024]{0:T(1024)S(1)} %get-tuple-element.73), kind=kCustom, calls=%fused_computation.5 | custom fusion | bytes 1180672 | tf_op jit(solution)/shard_map/gather | solution.py:151
  60.6 1.0 copy.139
  61.6 1.2 reshape.229
  63.2 1.3 copy.138
  64.6 1.1 reshape.228
  65.6 1.6 %copy.141 = f32[64,9,256]{0,2,1:T(8,128)S(1)} copy(f32[64,9,256]{2,1,0:T(8,128)} %reshape.228) | data formatting | bytes 1179648 | tf_op jit(solution)/shard_map/reshape | solution.py:151
  67.8 1.3 copy-done.3
  69.3 1.6 %multiply_add_fusion = f32[512,256]{0,1:T(8,128)S(1)} fusion(f32[512,256]{0,1:T(8,128)S(1)} %copy-done.6, f32[2,512,704]{1,2,0:T(8,128)S(1)} %copy-done.3, f32[64,256]{0,1:T(8,128)S(1)} %slice_reduce_fusion.1, f32[64,256]{0,1:T(8,128)S(1)} %slice_reduce_fusion.3, f32[64,256]{0,1:T(8,128)S(1)} %slice_bitcast_fusion.1), kind=kOutput, calls=%fused_computation.68 | convolution fusion | flops 1108492288 | bytes 3407872 | tf_op jit(solution)/shard_map/dot_general | solution.py:65
  74.4 2.3 %scatter_custom_fusion.3 = f32[576,64]{0,1:T(8,128)S(1)} fusion(s32[256]{0:T(256)S(1)} %bitcast.401, f32[256,576]{1,0:T(8,128)S(1)} %copy.144, f32[]{:T(128)} %constant.24.clone.1), kind=kCustom, calls=%fused_computation.142 | custom fusion | flops 147456 | bytes 147460 | tf_op jit(solution)/shard_map/scatter-add | solution.py:147
  76.6 2.3 %scatter_fusion.1 = f32[576,64]{0,1:T(8,128)S(1)} fusion(f32[576,64]{0,1:T(8,128)S(1)} %scatter_custom_fusion.3, s32[256]{0:T(256)S(1)} %bitcast.388, f32[256,576]{1,0:T(8,128)S(1)} %copy.145), kind=kCustom, calls=%fused_computation.13 | custom fusion | flops 147456 | bytes 1770496 | tf_op jit(solution)/shard_map/scatter-add | solution.py:147
  79.1 4.8 %collective-permute-start.13 = (f32[1,3,576,4]{2,3,1,0:T(4,128)S(1)}, f32[1,3,576,4]{2,3,1,0:T(4,128)S(1)}, u32[]{:S(2)}, u32[]{:S(2)}) collective-permute-start(f32[1,3,576,4]{2,3,1,0:T(4,128)S(1)} %get-tuple-element.34), channel_id=1, source_target_pairs={{4,0},{8,4},{12,8},{16,12},{20,16},{24,20},{28,24},{0,28},{5,1},{9... | collective-permute-start | bytes 82952 | tf_op jit(solution)/shard_map/ppermute | solution.py:21
  84.0 1.7 %collective-permute-done.12 = f32[1,3,576,4]{2,3,1,0:T(4,128)S(1)} collective-permute-done((f32[1,3,576,4]{2,3,1,0:T(4,128)S(1)}, f32[1,3,576,4]{2,3,1,0:T(4,128)S(1)}, u32[]{:S(2)}, u32[]{:S(2)}) %collective-permute-start.12) | collective-permute-done | bytes 27680 | tf_op jit(solution)/shard_map/ppermute | solution.py:20
  87.6 1.8 %collective-permute-done.14 = f32[5,1,576,4]{2,3,1,0:T(4,128)S(1)} collective-permute-done((f32[5,1,576,4]{2,3,1,0:T(4,128)S(1)}, f32[5,1,576,4]{2,3,1,0:T(4,128)S(1)}, u32[]{:S(2)}, u32[]{:S(2)}) %collective-permute-start.14) | collective-permute-done | bytes 46112 | tf_op jit(solution)/shard_map/ppermute | solution.py:20
  91.2 4.8 %collective-permute-start.17 = (f32[1,3,576,4]{2,3,1,0:T(4,128)S(1)}, f32[1,3,576,4]{2,3,1,0:T(4,128)S(1)}, u32[]{:S(2)}, u32[]{:S(2)}) collective-permute-start(f32[1,3,576,4]{2,3,1,0:T(4,128)S(1)} %get-tuple-element.30), channel_id=1, source_target_pairs={{4,0},{8,4},{12,8},{16,12},{20,16},{24,20},{28,24},{0,28},{5,1},{9... | collective-permute-start | bytes 82952 | tf_op jit(solution)/shard_map/ppermute | solution.py:21
  96.1 1.7 %collective-permute-done.16 = f32[1,3,576,4]{2,3,1,0:T(4,128)S(1)} collective-permute-done((f32[1,3,576,4]{2,3,1,0:T(4,128)S(1)}, f32[1,3,576,4]{2,3,1,0:T(4,128)S(1)}, u32[]{:S(2)}, u32[]{:S(2)}) %collective-permute-start.16) | collective-permute-done | bytes 27680 | tf_op jit(solution)/shard_map/ppermute | solution.py:20
  99.6 1.8 %collective-permute-done.18 = f32[5,1,576,4]{2,3,1,0:T(4,128)S(1)} collective-permute-done((f32[5,1,576,4]{2,3,1,0:T(4,128)S(1)}, f32[5,1,576,4]{2,3,1,0:T(4,128)S(1)}, u32[]{:S(2)}, u32[]{:S(2)}) %collective-permute-start.18) | collective-permute-done | bytes 46112 | tf_op jit(solution)/shard_map/ppermute | solution.py:20
  101.6 1.1 gather_fusion.6
  102.7 2.0 %gather_fusion.5 = f32[256,576]{1,0:T(8,128)} fusion(f32[576,64]{0,1:T(8,128)S(1)} %constant_dynamic-update-slice_fusion.42, s32[1024]{0:T(1024)S(1)} %get-tuple-element.73), kind=kCustom, calls=%fused_computation.7 | custom fusion | bytes 1180672 | tf_op jit(solution)/shard_map/gather | solution.py:151
  104.6 1.0 copy.147
  105.7 1.2 reshape.237
  107.3 1.3 copy.146
  108.6 1.1 reshape.236
  109.7 1.6 %copy.149 = f32[64,9,256]{0,2,1:T(8,128)S(1)} copy(f32[64,9,256]{2,1,0:T(8,128)} %reshape.236) | data formatting | bytes 1179648 | tf_op jit(solution)/shard_map/reshape | solution.py:151
  111.9 1.3 copy-done.4
  113.3 1.5 %fusion.9 = f32[512,256]{0,1:T(8,128)S(1)} fusion(f32[2,512,704]{1,2,0:T(8,128)S(1)} %copy-done.4, f32[64,256]{0,1:T(8,128)S(1)} %slice_reduce_fusion, f32[64,256]{0,1:T(8,128)S(1)} %slice_reduce_fusion.2, f32[64,256]{0,1:T(8,128)S(1)} %slice_bitcast_fusion, f32[512,256]{0,1:T(8,128)S(1)} %copy-done.2), kind=kOutput, calls=%fused_computation.25 | convolution fusion | flops 1107836928 | bytes 2883584 | tf_op jit(solution)/shard_map/dot_general | solution.py:65
  114.8 1.2 convolution_bitcast_fusion
  117.0 1.4 %scatter_custom_fusion.6 = f32[4,64]{0,1:T(8,128)S(1)} fusion(s32[256]{0:T(256)S(1)} %bitcast.402, f32[256,4]{1,0:T(8,128)S(1)} %copy.150, f32[]{:T(128)} %constant.24.clone.1), kind=kCustom, calls=%fused_computation.170 | custom fusion | flops 1024 | bytes 1028 | tf_op jit(solution)/shard_map/scatter-add | solution.py:159
  118.4 2.0 %scatter_fusion.2 = f32[4,64]{0,1:T(8,128)S(1)} fusion(f32[4,64]{0,1:T(8,128)S(1)} %scatter_custom_fusion.6, s32[256]{0:T(256)S(1)} %bitcast.389, f32[256,4]{1,0:T(8,128)S(1)} %copy.151), kind=kCustom, calls=%fused_computation.16 | custom fusion | flops 1024 | bytes 13312 | tf_op jit(solution)/shard_map/scatter-add | solution.py:160
  120.6 4.8 %collective-permute-start.21 = (f32[1,3,4,4]{3,2,1,0:T(4,128)S(1)}, f32[1,3,4,4]{3,2,1,0:T(4,128)S(1)}, u32[]{:S(2)}, u32[]{:S(2)}) collective-permute-start(f32[1,3,4,4]{3,2,1,0:T(4,128)S(1)} %bitcast.397), channel_id=1, source_target_pairs={{4,0},{8,4},{12,8},{16,12},{20,16},{24,20},{28,24},{0,28},{5,1},{9... | collective-permute-start | bytes 584 | tf_op jit(solution)/shard_map/ppermute | solution.py:21
  125.5 1.3 collective-permute-done.21
  126.8 5.0 %collective-permute-done.20 = f32[1,3,4,4]{3,2,1,0:T(4,128)S(1)} collective-permute-done((f32[1,3,4,4]{3,2,1,0:T(4,128)S(1)}, f32[1,3,4,4]{3,2,1,0:T(4,128)S(1)}, u32[]{:S(2)}, u32[]{:S(2)}) %collective-permute-start.20) | collective-permute-done | bytes 224 | tf_op jit(solution)/shard_map/ppermute | solution.py:20
  132.2 1.3 collective-permute-start.23
  133.5 1.4 collective-permute-done.22
  (229 shorter events, 33.6 us)
Async XLA Ops:
  0.6 114.2 %copy-start = (f32[512,512]{1,0:T(8,128)S(1)}, f32[512,512]{1,0:T(8,128)}, u32[]{:S(2)}) copy-start(f32[512,512]{1,0:T(8,128)} %param.27) | copy-start | bytes 3145732
  0.6 25.2 %copy-start.9 = (f32[512,8]{0,1:T(8,128)S(1)}, f32[512,8]{0,1:T(8,128)}, u32[]{:S(2)}) copy-start(f32[512,8]{0,1:T(8,128)} %param.22) | copy-start | bytes 49156
  5.3 7.4 %collective-permute-start.1 = (f32[1,3,4,4]{3,2,1,0:T(4,128)S(1)}, f32[1,3,4,4]{3,2,1,0:T(4,128)S(1)}, u32[]{:S(2)}, u32[]{:S(2)}) collective-permute-start(f32[1,3,4,4]{3,2,1,0:T(4,128)S(1)} %bitcast.394), channel_id=1, source_target_pairs={{4,0},{8,4},{12,8},{16,12},{20,16},{24,20},{28,24},{0,28},{5,1},{9... | collective-permute-start | bytes 584 | tf_op jit(solution)/shard_map/ppermute | solution.py:21
  11.4 6.3 %collective-permute-start = (f32[1,3,4,4]{3,2,1,0:T(4,128)S(1)}, f32[1,3,4,4]{3,2,1,0:T(4,128)S(1)}, u32[]{:S(2)}, u32[]{:S(2)}) collective-permute-start(f32[1,3,4,4]{3,2,1,0:T(4,128)S(1)} %bitcast.395), channel_id=1, source_target_pairs={{0,4},{4,8},{8,12},{12,16},{16,20},{20,24},{24,28},{28,0},{1,5},{5... | collective-permute-start | bytes 584 | tf_op jit(solution)/shard_map/ppermute | solution.py:20
  12.2 14.1 %copy-start.11 = (f32[512,8]{0,1:T(8,128)S(1)}, f32[512,8]{0,1:T(8,128)}, u32[]{:S(2)}) copy-start(f32[512,8]{0,1:T(8,128)} %param.23) | copy-start | bytes 49156
  17.7 3.1 %collective-permute-start.2 = (f32[5,1,4,4]{3,2,1,0:T(4,128)S(1)}, f32[5,1,4,4]{3,2,1,0:T(4,128)S(1)}, u32[]{:S(2)}, u32[]{:S(2)}) collective-permute-start(f32[5,1,4,4]{3,2,1,0:T(4,128)S(1)} %get-tuple-element.50), channel_id=1, source_target_pairs={{0,1},{1,2},{2,3},{3,0},{4,5},{5,6},{6,7},{7,4},{8,9},{9,10},{10,1... | collective-permute-start | bytes 968 | tf_op jit(solution)/shard_map/ppermute | solution.py:20
  18.6 3.2 %collective-permute-start.3 = (f32[5,1,4,4]{3,2,1,0:T(4,128)S(1)}, f32[5,1,4,4]{3,2,1,0:T(4,128)S(1)}, u32[]{:S(2)}, u32[]{:S(2)}) collective-permute-start(f32[5,1,4,4]{3,2,1,0:T(4,128)S(1)} %get-tuple-element.49), channel_id=1, source_target_pairs={{1,0},{2,1},{3,2},{0,3},{5,4},{6,5},{7,6},{4,7},{9,8},{10,9},{11,1... | collective-permute-start | bytes 968 | tf_op jit(solution)/shard_map/ppermute | solution.py:21
  26.3 1.3 copy-start.7
  26.9 0.8 copy-start.5
  35.1 6.6 %collective-permute-start.4 = (f32[1,3,576,4]{2,3,1,0:T(4,128)S(1)}, f32[1,3,576,4]{2,3,1,0:T(4,128)S(1)}, u32[]{:S(2)}, u32[]{:S(2)}) collective-permute-start(f32[1,3,576,4]{2,3,1,0:T(4,128)S(1)} %get-tuple-element.41), channel_id=1, source_target_pairs={{0,4},{4,8},{8,12},{12,16},{16,20},{20,24},{24,28},{28,0},{1,5},{5... | collective-permute-start | bytes 82952 | tf_op jit(solution)/shard_map/ppermute | solution.py:20
  35.2 6.6 %collective-permute-start.5 = (f32[1,3,576,4]{2,3,1,0:T(4,128)S(1)}, f32[1,3,576,4]{2,3,1,0:T(4,128)S(1)}, u32[]{:S(2)}, u32[]{:S(2)}) collective-permute-start(f32[1,3,576,4]{2,3,1,0:T(4,128)S(1)} %get-tuple-element.42), channel_id=1, source_target_pairs={{4,0},{8,4},{12,8},{16,12},{20,16},{24,20},{28,24},{0,28},{5,1},{9... | collective-permute-start | bytes 82952 | tf_op jit(solution)/shard_map/ppermute | solution.py:21
  41.8 3.6 %collective-permute-start.6 = (f32[5,1,576,4]{2,3,1,0:T(4,128)S(1)}, f32[5,1,576,4]{2,3,1,0:T(4,128)S(1)}, u32[]{:S(2)}, u32[]{:S(2)}) collective-permute-start(f32[5,1,576,4]{2,3,1,0:T(4,128)S(1)} %get-tuple-element.28), channel_id=1, source_target_pairs={{0,1},{1,2},{2,3},{3,0},{4,5},{5,6},{6,7},{7,4},{8,9},{9,10},{10,1... | collective-permute-start | bytes 138248 | tf_op jit(solution)/shard_map/ppermute | solution.py:20
  42.3 3.1 %collective-permute-start.7 = (f32[5,1,576,4]{2,3,1,0:T(4,128)S(1)}, f32[5,1,576,4]{2,3,1,0:T(4,128)S(1)}, u32[]{:S(2)}, u32[]{:S(2)}) collective-permute-start(f32[5,1,576,4]{2,3,1,0:T(4,128)S(1)} %get-tuple-element.27), channel_id=1, source_target_pairs={{1,0},{2,1},{3,2},{0,3},{5,4},{6,5},{7,6},{4,7},{9,8},{10,9},{11,1... | collective-permute-start | bytes 138248 | tf_op jit(solution)/shard_map/ppermute | solution.py:21
  47.1 6.7 %collective-permute-start.8 = (f32[1,3,576,4]{2,3,1,0:T(4,128)S(1)}, f32[1,3,576,4]{2,3,1,0:T(4,128)S(1)}, u32[]{:S(2)}, u32[]{:S(2)}) collective-permute-start(f32[1,3,576,4]{2,3,1,0:T(4,128)S(1)} %get-tuple-element.37), channel_id=1, source_target_pairs={{0,4},{4,8},{8,12},{12,16},{16,20},{20,24},{24,28},{28,0},{1,5},{5... | collective-permute-start | bytes 82952 | tf_op jit(solution)/shard_map/ppermute | solution.py:20
  47.2 6.6 %collective-permute-start.9 = (f32[1,3,576,4]{2,3,1,0:T(4,128)S(1)}, f32[1,3,576,4]{2,3,1,0:T(4,128)S(1)}, u32[]{:S(2)}, u32[]{:S(2)}) collective-permute-start(f32[1,3,576,4]{2,3,1,0:T(4,128)S(1)} %get-tuple-element.38), channel_id=1, source_target_pairs={{4,0},{8,4},{12,8},{16,12},{20,16},{24,20},{28,24},{0,28},{5,1},{9... | collective-permute-start | bytes 82952 | tf_op jit(solution)/shard_map/ppermute | solution.py:21
  53.8 3.6 %collective-permute-start.10 = (f32[5,1,576,4]{2,3,1,0:T(4,128)S(1)}, f32[5,1,576,4]{2,3,1,0:T(4,128)S(1)}, u32[]{:S(2)}, u32[]{:S(2)}) collective-permute-start(f32[5,1,576,4]{2,3,1,0:T(4,128)S(1)} %get-tuple-element.26), channel_id=1, source_target_pairs={{0,1},{1,2},{2,3},{3,0},{4,5},{5,6},{6,7},{7,4},{8,9},{9,10},{10,1... | collective-permute-start | bytes 138248 | tf_op jit(solution)/shard_map/ppermute | solution.py:20
  54.6 2.9 %collective-permute-start.11 = (f32[5,1,576,4]{2,3,1,0:T(4,128)S(1)}, f32[5,1,576,4]{2,3,1,0:T(4,128)S(1)}, u32[]{:S(2)}, u32[]{:S(2)}) collective-permute-start(f32[5,1,576,4]{2,3,1,0:T(4,128)S(1)} %get-tuple-element.25), channel_id=1, source_target_pairs={{1,0},{2,1},{3,2},{0,3},{5,4},{6,5},{7,6},{4,7},{9,8},{10,9},{11,1... | collective-permute-start | bytes 138248 | tf_op jit(solution)/shard_map/ppermute | solution.py:21
  65.6 1.6 %copy-start.10 = (f32[9]{0:T(128)S(1)}, f32[9]{0:T(128)}, u32[]{:S(2)}) copy-start(f32[9]{0:T(128)} %constant.68.clone) | copy-start | bytes 112
  67.3 1.8 %copy-start.3 = (f32[2,512,704]{1,2,0:T(8,128)S(1)}, f32[2,512,704]{1,2,0:T(8,128)}, u32[]{:S(2)}) copy-start(f32[2,512,704]{1,2,0:T(8,128)} %param.26) | copy-start | bytes 8650756
  67.7 1.6 %copy-start.6 = (f32[512,256]{0,1:T(8,128)S(1)}, f32[512,256]{0,1:T(8,128)}, u32[]{:S(2)}) copy-start(f32[512,256]{0,1:T(8,128)} %copy-done.5) | copy-start | bytes 1572868
  69.3 2.4 %copy-start.8 = (f32[2,64,512]{2,1,0:T(8,128)S(1)}, f32[2,64,512]{2,1,0:T(8,128)}, u32[]{:S(2)}) copy-start(f32[2,64,512]{2,1,0:T(8,128)} %param.25) | copy-start | bytes 786436
  70.9 0.8 copy-start.1
  79.1 6.7 %collective-permute-start.12 = (f32[1,3,576,4]{2,3,1,0:T(4,128)S(1)}, f32[1,3,576,4]{2,3,1,0:T(4,128)S(1)}, u32[]{:S(2)}, u32[]{:S(2)}) collective-permute-start(f32[1,3,576,4]{2,3,1,0:T(4,128)S(1)} %get-tuple-element.33), channel_id=1, source_target_pairs={{0,4},{4,8},{8,12},{12,16},{16,20},{20,24},{24,28},{28,0},{1,5},{5... | collective-permute-start | bytes 82952 | tf_op jit(solution)/shard_map/ppermute | solution.py:20
  79.1 6.6 %collective-permute-start.13 = (f32[1,3,576,4]{2,3,1,0:T(4,128)S(1)}, f32[1,3,576,4]{2,3,1,0:T(4,128)S(1)}, u32[]{:S(2)}, u32[]{:S(2)}) collective-permute-start(f32[1,3,576,4]{2,3,1,0:T(4,128)S(1)} %get-tuple-element.34), channel_id=1, source_target_pairs={{4,0},{8,4},{12,8},{16,12},{20,16},{24,20},{28,24},{0,28},{5,1},{9... | collective-permute-start | bytes 82952 | tf_op jit(solution)/shard_map/ppermute | solution.py:21
  85.8 3.6 %collective-permute-start.14 = (f32[5,1,576,4]{2,3,1,0:T(4,128)S(1)}, f32[5,1,576,4]{2,3,1,0:T(4,128)S(1)}, u32[]{:S(2)}, u32[]{:S(2)}) collective-permute-start(f32[5,1,576,4]{2,3,1,0:T(4,128)S(1)} %get-tuple-element.24), channel_id=1, source_target_pairs={{0,1},{1,2},{2,3},{3,0},{4,5},{5,6},{6,7},{7,4},{8,9},{9,10},{10,1... | collective-permute-start | bytes 138248 | tf_op jit(solution)/shard_map/ppermute | solution.py:20
  86.5 2.8 %collective-permute-start.15 = (f32[5,1,576,4]{2,3,1,0:T(4,128)S(1)}, f32[5,1,576,4]{2,3,1,0:T(4,128)S(1)}, u32[]{:S(2)}, u32[]{:S(2)}) collective-permute-start(f32[5,1,576,4]{2,3,1,0:T(4,128)S(1)} %get-tuple-element.23), channel_id=1, source_target_pairs={{1,0},{2,1},{3,2},{0,3},{5,4},{6,5},{7,6},{4,7},{9,8},{10,9},{11,1... | collective-permute-start | bytes 138248 | tf_op jit(solution)/shard_map/ppermute | solution.py:21
  91.1 6.7 %collective-permute-start.16 = (f32[1,3,576,4]{2,3,1,0:T(4,128)S(1)}, f32[1,3,576,4]{2,3,1,0:T(4,128)S(1)}, u32[]{:S(2)}, u32[]{:S(2)}) collective-permute-start(f32[1,3,576,4]{2,3,1,0:T(4,128)S(1)} %get-tuple-element.29), channel_id=1, source_target_pairs={{0,4},{4,8},{8,12},{12,16},{16,20},{20,24},{24,28},{28,0},{1,5},{5... | collective-permute-start | bytes 82952 | tf_op jit(solution)/shard_map/ppermute | solution.py:20
  91.2 6.6 %collective-permute-start.17 = (f32[1,3,576,4]{2,3,1,0:T(4,128)S(1)}, f32[1,3,576,4]{2,3,1,0:T(4,128)S(1)}, u32[]{:S(2)}, u32[]{:S(2)}) collective-permute-start(f32[1,3,576,4]{2,3,1,0:T(4,128)S(1)} %get-tuple-element.30), channel_id=1, source_target_pairs={{4,0},{8,4},{12,8},{16,12},{20,16},{24,20},{28,24},{0,28},{5,1},{9... | collective-permute-start | bytes 82952 | tf_op jit(solution)/shard_map/ppermute | solution.py:21
  97.8 3.6 %collective-permute-start.18 = (f32[5,1,576,4]{2,3,1,0:T(4,128)S(1)}, f32[5,1,576,4]{2,3,1,0:T(4,128)S(1)}, u32[]{:S(2)}, u32[]{:S(2)}) collective-permute-start(f32[5,1,576,4]{2,3,1,0:T(4,128)S(1)} %get-tuple-element.22), channel_id=1, source_target_pairs={{0,1},{1,2},{2,3},{3,0},{4,5},{5,6},{6,7},{7,4},{8,9},{9,10},{10,1... | collective-permute-start | bytes 138248 | tf_op jit(solution)/shard_map/ppermute | solution.py:20
  98.8 2.7 %collective-permute-start.19 = (f32[5,1,576,4]{2,3,1,0:T(4,128)S(1)}, f32[5,1,576,4]{2,3,1,0:T(4,128)S(1)}, u32[]{:S(2)}, u32[]{:S(2)}) collective-permute-start(f32[5,1,576,4]{2,3,1,0:T(4,128)S(1)} %get-tuple-element.21), channel_id=1, source_target_pairs={{1,0},{2,1},{3,2},{0,3},{5,4},{6,5},{7,6},{4,7},{9,8},{10,9},{11,1... | collective-permute-start | bytes 138248 | tf_op jit(solution)/shard_map/ppermute | solution.py:21
  111.3 1.8 %copy-start.4 = (f32[2,512,704]{1,2,0:T(8,128)S(1)}, f32[2,512,704]{1,2,0:T(8,128)}, u32[]{:S(2)}) copy-start(f32[2,512,704]{1,2,0:T(8,128)} %param.26) | copy-start | bytes 8650756
  111.7 1.6 %copy-start.2 = (f32[512,256]{0,1:T(8,128)S(1)}, f32[512,256]{0,1:T(8,128)}, u32[]{:S(2)}) copy-start(f32[512,256]{0,1:T(8,128)} %copy-done.1) | copy-start | bytes 1572868
  114.8 1.2 copy-start.12
  120.6 6.2 %collective-permute-start.21 = (f32[1,3,4,4]{3,2,1,0:T(4,128)S(1)}, f32[1,3,4,4]{3,2,1,0:T(4,128)S(1)}, u32[]{:S(2)}, u32[]{:S(2)}) collective-permute-start(f32[1,3,4,4]{3,2,1,0:T(4,128)S(1)} %bitcast.397), channel_id=1, source_target_pairs={{4,0},{8,4},{12,8},{16,12},{20,16},{24,20},{28,24},{0,28},{5,1},{9... | collective-permute-start | bytes 584 | tf_op jit(solution)/shard_map/ppermute | solution.py:21
  125.4 6.3 %collective-permute-start.20 = (f32[1,3,4,4]{3,2,1,0:T(4,128)S(1)}, f32[1,3,4,4]{3,2,1,0:T(4,128)S(1)}, u32[]{:S(2)}, u32[]{:S(2)}) collective-permute-start(f32[1,3,4,4]{3,2,1,0:T(4,128)S(1)} %bitcast.396), channel_id=1, source_target_pairs={{0,4},{4,8},{8,12},{12,16},{16,20},{20,24},{24,28},{28,0},{1,5},{5... | collective-permute-start | bytes 584 | tf_op jit(solution)/shard_map/ppermute | solution.py:20
  131.7 3.1 %collective-permute-start.22 = (f32[5,1,4,4]{3,2,1,0:T(4,128)S(1)}, f32[5,1,4,4]{3,2,1,0:T(4,128)S(1)}, u32[]{:S(2)}, u32[]{:S(2)}) collective-permute-start(f32[5,1,4,4]{3,2,1,0:T(4,128)S(1)} %get-tuple-element.48), channel_id=1, source_target_pairs={{0,1},{1,2},{2,3},{3,0},{4,5},{5,6},{6,7},{7,4},{8,9},{9,10},{10,1... | collective-permute-start | bytes 968 | tf_op jit(solution)/shard_map/ppermute | solution.py:20
  132.2 2.7 %collective-permute-start.23 = (f32[5,1,4,4]{3,2,1,0:T(4,128)S(1)}, f32[5,1,4,4]{3,2,1,0:T(4,128)S(1)}, u32[]{:S(2)}, u32[]{:S(2)}) collective-permute-start(f32[5,1,4,4]{3,2,1,0:T(4,128)S(1)} %get-tuple-element.47), channel_id=1, source_target_pairs={{1,0},{2,1},{3,2},{0,3},{5,4},{6,5},{7,6},{4,7},{9,8},{10,9},{11,1... | collective-permute-start | bytes 968 | tf_op jit(solution)/shard_map/ppermute | solution.py:21
where the time goes:
time: 139 us; the launch traced here: 137 us
  starting transfers between devices  41.1 us (30%)
  local copies, waits for them, and re-layouts  35.5 us (26%)
  waiting for transfers between devices  28.5 us (21%)
  other arithmetic  21.5 us (15%)
  matrix products  8.4 us (6%)
  between operations  2.26 us (2%)
    ppermute x12, starting transfers between devices, extended(): after = lax.ppermute(initial, axis, down)  37.5 us
    ppermute x12, waiting for transfers between devices, extended(): before = lax.ppermute(last, axis, up)  25.8 us
    scatter-add x4, other arithmetic, local(): partial_value.at[:, centre].add(contrib).at[:, other]  9.15 us
    gather x4, local copies, waits for them, and re-layouts, local(): env_centre = env_pool[:, centre].reshape(channels, 9, count_edges)  6.51 us
    unnamed x72, local copies, waits for them, and re-layouts  6.24 us
    reshape x4, local copies, waits for them, and re-layouts, local(): env_centre = env_pool[:, centre].reshape(channels, 9, count_edges)  5.41 us
    gather x4, local copies, waits for them, and re-layouts, local(): env_other = env_pool[:, other].reshape(channels, 9, count_edges)  4.28 us
    ppermute x12, starting transfers between devices, extended(): before = lax.ppermute(last, axis, up)  3.66 us
  transfers between devices with their start and end apart: 24, of which 15 were waited for; matrix products, arithmetic and copies ran while one was open for 1% of the time, Pallas kernels for 0%

commit v1 on v0

v1 whole, which is shorter than its diff:
```python
import functools
import math

import jax
import jax.numpy as jnp
import numpy as np
from jax import lax
from jax.experimental import pallas as pl
from jax.experimental.pallas import tpu as pltpu
from jax.sharding import PartitionSpec as P

offset_x = (-1, -1, -1, 0, 0, 1, 1, 1)
offset_y = (-1, 0, 1, -1, 1, -1, 0, 1)
f32 = jnp.float32
bf16 = jnp.bfloat16
highest = lax.Precision.HIGHEST
order = (0, 4, 5, 6, 7, 8, 1, 2, 3)
even_count = 6
ATOMS = 32
LANES = 128


def folded(position, length):
    if length % 2:
        return position
    half = length // 2
    return 2 * position if position < half else 2 * (length - 1 - position) + 1


class Layout:
    def __init__(self, size_x, size_y):
        self.size_x, self.size_y = size_x, size_y
        self.count = size_x * size_y
        self.device = np.zeros((size_x, size_y), np.int32)
        self.domain = np.zeros((self.count, 2), np.int32)
        for x in range(size_x):
            for y in range(size_y):
                at = folded(x, size_x) * size_y + y
                self.device[x, y] = at
                self.domain[at] = (x, y)

    def home(self, x, y):
        return (x % self.size_x) * self.size_y + y % self.size_y

    def shift(self, step_x, step_y):
        pairs = []
        for x in range(self.size_x):
            for y in range(self.size_y):
                target = self.device[(x + step_x) % self.size_x, (y + step_y) % self.size_y]
                pairs.append((int(self.device[x, y]), int(target)))
        return pairs

    def position(self):
        here = (lax.axis_index("gx"), lax.axis_index("gy"))
        return (here, (unfolded(here[0], self.size_x), here[1]))

    def at_home(self, x, y):
        return wrapped(x, self.size_x) * self.size_y + wrapped(y, self.size_y)

    def at_work(self, x, y):
        x = traced_fold(wrapped(x, self.size_x), self.size_x)
        return x * self.size_y + wrapped(y, self.size_y)


def wrapped(value, length):
    return lax.rem(value + length, length)


def unfolded(at, length):
    if length % 2:
        return at
    return jnp.where(at % 2 == 0, at // 2, length - 1 - at // 2)


def traced_fold(position, length):
    if length % 2:
        return position
    return jnp.where(position < length // 2, 2 * position, 2 * (length - 1 - position) + 1)


def split(value):
    top = value.astype(bf16)
    return (top, (value - top.astype(f32)).astype(bf16))


def mm(left, right, contract=((1,), (0,))):
    return lax.dot_general(left, right, (contract, ((), ())), preferred_element_type=f32)


def dot3(left_top, left_rest, right):
    right_top, right_rest = split(right)
    return mm(left_top, right_top) + (mm(left_top, right_rest) + mm(left_rest, right_top))


def dot_stacked(halves, rows, right):
    right_top, right_rest = split(right)
    both = mm(halves, right_top)
    return both[:rows] + (both[rows : 2 * rows] + mm(halves[:rows], right_rest))


def exact(left, right, contract=((1,), (0,))):
    rows = left.shape[0]
    top = left.astype(bf16).astype(f32)
    rest = left - top
    middle = rest.astype(bf16).astype(f32)
    parts = jnp.concatenate([top, middle, rest - middle], axis=0).astype(bf16)
    parts = mm(parts, right, contract)
    return parts[:rows] + (parts[rows : 2 * rows] + parts[2 * rows :])


def silu(value):
    half = 0.5 * value
    return half + half * jnp.tanh(half)


def iota(shape, dim):
    return lax.broadcasted_iota(jnp.int32, shape, dim)


def edge_rows(static):
    centre = jnp.concatenate([static[2:3], static[3:4]], axis=1).astype(jnp.int32)
    other = jnp.concatenate([static[4:5], static[5:6]], axis=1).astype(jnp.int32)
    ghost = jnp.bitwise_xor(other - ATOMS, 28) + ATOMS
    return (centre, jnp.where(other >= ATOMS, ghost, other))


def onehots(static):
    centre, other = edge_rows(static)
    slots = iota((2 * ATOMS, centre.shape[1]), 0)
    return ((slots == centre).astype(f32), (slots == other).astype(f32))


def incidence(at_centre, at_other):
    return ((at_centre + at_other).astype(bf16), (at_centre - at_other).astype(bf16))


def send_columns(row):
    return (iota((ATOMS, ATOMS), 0) == row[:, :ATOMS].astype(jnp.int32)).astype(bf16)


def pick_rows(rows):
    entry = (iota(rows.shape, 1) % ATOMS) // 4
    return jnp.sum(jnp.where(entry == iota(rows.shape, 0), rows, 0.0), axis=0, keepdims=True)


def stacked_features(basis, kind_centre, kind_other):
    top = basis.astype(bf16).astype(f32)
    kinds = [kind_centre, kind_other]
    stacked = [top, basis - top, top] + kinds + kinds + [jnp.zeros_like(basis)]
    return jnp.concatenate(stacked, axis=0).astype(bf16)


def contributions(hidden, env_halves, harm, factor):
    weights = dot_stacked(env_halves, env_halves.shape[0] // 2, hidden) * (0.25 * factor)
    terms = [weights * harm[m] for m in order]
    return [split(jnp.concatenate(g, axis=0)) for g in (terms[:even_count], terms[even_count:])]


def scatter(terms, picks):
    last = ((1,), (1,))
    sides = [mm(pick, top, last) + mm(pick, rest, last) for pick, (top, rest) in zip(picks, terms)]
    return jnp.concatenate(sides, axis=1)


def store_sides(items, up_ref, mid_ref, down_ref):
    for i in range(3):
        up_ref[i] = items[4 * i : 4 * i + 4]
    for i in range(2):
        mid_ref[i] = items[12 + 4 * i : 16 + 4 * i]
    for i in range(3):
        down_ref[i] = items[20 + 4 * i : 24 + 4 * i]


def load_sides(dest, base, before_ref, after_ref, up_ref, down_ref):
    for i, k in enumerate((0, 3, 5)):
        dest[base + 4 * k : base + 4 * k + 4, :] = before_ref[i]
    for i, k in enumerate((2, 4, 7)):
        dest[base + 4 * k : base + 4 * k + 4, :] = after_ref[i]
    dest[base + 4 : base + 8, :] = up_ref[1]
    dest[base + 24 : base + 28, :] = down_ref[1]


def fetch(sources, targets, semaphores):
    copies = [
        pltpu.make_async_copy(source, target, semaphores.at[i])
        for i, (source, target) in enumerate(zip(sources, targets))
    ]
    for copy in copies:
        copy.start()
    return copies


def static_kernel(*refs):
    sources, copies_ref, targets, semaphores = (refs[:5], refs[5], refs[6:11], refs[11])
    for copy in fetch(sources, targets, semaphores):
        copy.wait()
    count_ref, positions_ref, species_ref, sends_ref, edges_ref = targets
    atoms = jnp.concatenate([positions_ref[...], species_ref[...].astype(f32)], axis=0)
    lane = iota((ATOMS, LANES), 1)
    spread = (iota((ATOMS, LANES), 0) == lane % ATOMS).astype(bf16)
    atoms = jnp.concatenate([atoms, atoms], axis=0)
    part = iota((8, LANES), 1) // ATOMS == iota((8, LANES), 0)
    atoms = jnp.sum(jnp.where(part, exact(atoms, spread), 0.0), axis=0, keepdims=True)
    sends = sends_ref[...].astype(f32)
    sends = jnp.concatenate([sends, sends], axis=0)
    lane = iota((8, LANES), 1)
    spread = (iota((8, LANES), 0) == lane % ATOMS // 4).astype(bf16)
    entry = mm(sends.astype(bf16), spread)
    entry = jnp.where(lane % 4 == iota((8, LANES), 0), entry, 0.0)
    sends = jnp.sum(entry, axis=0, keepdims=True)
    edges = edges_ref[...].astype(f32)
    count = jnp.broadcast_to(count_ref[...].astype(f32), (2, LANES))
    block = jnp.concatenate(
        [
            atoms,
            sends,
            edges[0:1, :LANES],
            edges[0:1, LANES:],
            edges[1:2, :LANES],
            edges[1:2, LANES:],
            count,
        ],
        axis=0,
    )
    copies_ref[...] = jnp.broadcast_to(block[None], copies_ref.shape)


def weights_kernel(*refs):
    sources, outs, targets, semaphores = (refs[:6], refs[6:9], refs[9:15], refs[15])
    latent_top_ref, latent_rest_ref, small_ref = outs
    latent_ref, env_ref, radial_ref, centre_ref, neighbour_ref, head_ref = targets
    for copy in fetch(sources, targets, semaphores):
        copy.wait()
    for layer in range(latent_ref.shape[0]):
        top, rest = split(latent_ref[layer].T)
        latent_top_ref[layer] = top
        latent_rest_ref[layer] = rest
        top, rest = split(env_ref[layer])
        small_ref[layer] = jnp.concatenate([top, rest], axis=0)

    def halves(value):
        top = value.astype(bf16).astype(f32)
        return (top, value - top)

    radial, centre, neighbour = (halves(r[...]) for r in (radial_ref, centre_ref, neighbour_ref))
    stacked = [radial[0], radial[0], radial[1], centre[0], neighbour[0], centre[1], neighbour[1]]
    top, rest = halves(head_ref[...])
    zeros = jnp.zeros((60, top.shape[1]), f32)
    stacked = stacked + [jnp.zeros_like(radial[0]), top, rest, zeros]
    small_ref[env_ref.shape[0]] = jnp.concatenate(stacked, axis=0).astype(bf16)


def lane_pick(rows, index):
    return jnp.take_along_axis(rows, index, axis=1, mode="promise_in_bounds")


def geometry(dx, dy, dz):
    squared = dx * dx + dy * dy + dz * dz
    scale = 1.0 / jnp.sqrt(1.0 + squared)
    x, y, z = dx * scale, dy * scale, dz * scale
    root = math.sqrt(3.0)
    harm = [
        jnp.ones_like(x),
        x,
        y,
        z,
        root * x * y,
        root * y * z,
        0.5 * (3.0 * z * z - 1.0),
        root * x * z,
        0.5 * root * (x * x - y * y),
    ]
    return ((x, y, z), jnp.sqrt(squared), harm)


def first_hidden(length, kind_centre, kind_other, embed):
    rows = iota((8, length.shape[1]), 0)
    basis = jnp.exp(-2.0 * (length - 0.5 * rows.astype(f32)) ** 2)
    kinds = [(rows == (kind + 0.5).astype(jnp.int32)).astype(f32) for kind in (kind_centre, kind_other)]
    return silu(mm(embed, stacked_features(basis, *kinds)))


def near_offsets(length, reach):
    offsets, seen = ([], set())
    for distance in range(reach + 1):
        for offset in (distance, -distance):
            if offset % length not in seen:
                seen.add(offset % length)
                offsets.append(offset)
    return offsets


def near_domains(layout, reach):
    found = [
        (x, y) for x in near_offsets(layout.size_x, reach) for y in near_offsets(layout.size_y, reach)
    ]
    return sorted(found, key=lambda at: max(abs(at[0]), abs(at[1])))


def look_up(gathered_ref, home_of, offset):
    home = home_of(*offset)
    static = gathered_ref[home]
    around = [home_of(offset[0] - offset_x[k], offset[1] - offset_y[k]) for k in range(8)]
    nearby = [gathered_ref[at] for at in around]
    lane = iota((8, LANES), 1)
    row = iota((8, LANES), 0)
    group = lane % ATOMS // 4
    sends = pick_rows(jnp.concatenate([tile[1:2] for tile in nearby], axis=0))
    sends = jnp.broadcast_to(sends, (8, LANES)).astype(jnp.int32)
    atoms = jnp.concatenate([tile[0:1] for tile in nearby], axis=0)
    ghosts = pick_rows(lane_pick(atoms, lane // ATOMS * ATOMS + sends))
    ghosts = jnp.broadcast_to(ghosts, (8, LANES))
    owner = jnp.zeros((8, LANES), jnp.int32)
    for k in range(8):
        owner = jnp.where(group == k, around[k], owner)
    entries = (owner * ATOMS + sends + 1).astype(f32)
    own = jnp.broadcast_to(static[0:1], (8, LANES))
    first = row % 4 * ATOMS
    tiles = []
    for half in range(2):
        centre = jnp.broadcast_to(static[2 + half : 3 + half], (8, LANES)).astype(jnp.int32)
        other = jnp.broadcast_to(static[4 + half : 5 + half], (8, LANES)).astype(jnp.int32)
        place = jnp.bitwise_and(other, ATOMS - 1)
        entry = jnp.bitwise_xor(place, 28)
        outside = other >= ATOMS
        start = lane_pick(own, first + centre)
        finish = jnp.where(outside, lane_pick(ghosts, first + entry), lane_pick(own, first + place))
        at_start = (home * ATOMS + 1 + centre).astype(f32)
        at_finish = jnp.where(
            outside, lane_pick(entries, entry), (home * ATOMS + 1 + place).astype(f32)
        )
        tile = jnp.where(row < 3, finish - start, finish)
        tile = jnp.where(row == 3, start, tile)
        tile = jnp.where(row == 4, at_start, tile)
        tile = jnp.where(row == 5, at_finish, tile)
        live = (lane + half * LANES < 2 * LANES // ATOMS * static[6:7].astype(jnp.int32)).astype(f32)
        tiles.append(jnp.where(row == 6, live, tile))
    return (tiles, entries, static)


def pack(rows_ref, chosen_ref, packed_ref, count):
    chosen = chosen_ref[...]
    mask = chosen.astype(bf16)
    padded = chosen.shape[0]
    before = (iota((LANES, LANES), 0) <= iota((LANES, LANES), 1)).astype(bf16)
    place = (mm(mask, before) - 1.0).astype(jnp.int32)
    totals = mm(mask, jnp.ones((LANES, LANES), bf16))
    above = (iota((padded, padded), 0) > iota((padded, padded), 1)).astype(bf16)
    starts = mm(above, totals.astype(bf16))
    packed_ref[...] = jnp.zeros_like(packed_ref)
    source = iota(chosen.shape, 1)
    distance = jnp.where(chosen > 0, source - place, 0)
    for step in range(7):
        bit = 1 << step
        coming = pltpu.roll(distance, LANES - bit, 1)
        arrives = jnp.bitwise_and(coming, bit) != 0
        source = jnp.where(arrives, pltpu.roll(source, LANES - bit, 1), source)
        stays = jnp.where(jnp.bitwise_and(distance, bit) != 0, 0, distance)
        distance = jnp.where(arrives, coming, stays)
    taken = totals.astype(jnp.int32)
    lane = iota((8, LANES), 1)
    for i in range(count):
        moved = lane_pick(rows_ref[i], jnp.broadcast_to(source[i : i + 1], (8, LANES)))
        moved = jnp.where(lane < taken[i : i + 1], moved, 0.0)
        start = jnp.max(starts[i : i + 1]).astype(jnp.int32)
        shift = jnp.bitwise_and(start, LANES - 1)
        block = lax.shift_right_logical(start, 7)
        moved = pltpu.roll(moved, shift, 1)
        packed_ref[block] += jnp.where(lane >= shift, moved, 0.0)
        packed_ref[block + 1] += jnp.where(lane < shift, moved, 0.0)
    return jnp.max(starts[padded - 1 :] + totals[padded - 1 :]).astype(jnp.int32)


def env_scalars(even, odd, harm):
    blocks = [even[64 * i : 64 * i + 64] for i in range(even_count)]
    blocks += [odd[64 * i : 64 * i + 64] for i in range(3)]
    product = {m: blocks[i] * harm[m] for i, m in enumerate(order)}
    return jnp.concatenate(
        [
            product[0],
            product[1] + product[2] + product[3],
            product[4] + product[5] + product[6] + product[7] + product[8],
        ],
        axis=0,
    )


def refined(hidden, ahead, pool, harm, sums, weight_top, weight_rest):
    top, rest = split(pool)
    first = ((0,), (0,))
    width = 64 * even_count
    even = mm(top[:, :width], sums[0], first) + mm(rest[:, :width], sums[0], first)
    odd = mm(top[:, width:], sums[1], first) + mm(rest[:, width:], sums[1], first)
    return hidden + silu(ahead + dot3(weight_top, weight_rest, env_scalars(even, odd, harm)))


def front_kernel(
    layout,
    gathered_ref,
    small_ref,
    top_ref,
    rest_ref,
    hidden_ref,
    geo_ref,
    static_ref,
    home_ref,
    env_ref,
    up_ref,
    mid_ref,
    down_ref,
    rows_ref,
    chosen_ref,
    packed_ref,
    pool_ref,
    coming_ref,
    packed_in_ref,
    slots_ref,
    pool_in_ref,
):
    (here_x, here_y), (at_x, at_y) = layout.position()
    home_ref[...] = gathered_ref[layout.at_home(here_x, here_y)]

    def home_of(x, y):
        return layout.at_home(at_x + x, at_y + y)

    tiles, entries, static = look_up(gathered_ref, home_of, (0, 0))
    static_ref[...] = static
    lane = iota((1, LANES), 1)
    first_atom = home_of(0, 0) * ATOMS + 1
    slots = jnp.where(lane < ATOMS, (first_atom + lane).astype(f32), entries[0:1])
    slots = jnp.broadcast_to(slots, (LANES, LANES)).T[: 2 * ATOMS]

    named = [jnp.where(slots[ATOMS:] == tile[5:6], tile[6:7], 0.0) for tile in tiles]
    named = jnp.max(jnp.maximum(*named), axis=1, keepdims=True) > 0
    slots = jnp.concatenate([slots[:ATOMS], jnp.where(named, slots[ATOMS:], -1.0)], axis=0)

    def touches(slots, tile):
        found = jnp.where((slots == tile[4:5]) | (slots == tile[5:6]), 1.0, 0.0)
        return jnp.max(found, axis=0, keepdims=True)

    chosen_ref[...] = jnp.zeros_like(chosen_ref)
    domains = near_domains(layout, 2)
    rows = 2 * len(domains) - 2
    rows_in = coming_ref.shape[0]
    for i, offset in enumerate(domains[1:]):
        others, _, _ = look_up(gathered_ref, home_of, offset)
        for half, tile in enumerate(others):
            at = 2 * i + half
            rows_ref[at] = tile
            if at < rows_in:
                place = tile[5:6].astype(jnp.int32) - first_atom
                coming = jnp.where((place >= 0) & (place < ATOMS), tile[6:7], 0.0)
                coming_ref[at : at + 1, :] = coming
    count_in = pack(rows_ref, coming_ref, packed_in_ref, rows_in)
    tiles_in = lax.shift_right_logical(count_in + LANES - 1, 7)

    incoming = packed_in_ref[0]
    slots = jnp.concatenate([slots, jnp.broadcast_to(incoming[4:5], (LANES, LANES)).T], axis=0)

    def choose(slots):
        for at in range(rows):
            tile = rows_ref[at]
            live = tile[6:7] - coming_ref[at : at + 1, :] if at < rows_in else tile[6:7]
            row = slice(at, at + 1)
            chosen_ref[row, :] = jnp.maximum(chosen_ref[row, :], touches(slots, tile) * live)

    choose(slots)

    def add_slots(tile, carry):
        ids = jnp.broadcast_to(packed_in_ref[tile][4:5], (LANES, LANES)).T
        slots_ref[tile] = ids
        choose(ids)
        return carry

    lax.fori_loop(1, tiles_in, add_slots, 0)
    count = pack(rows_ref, chosen_ref, packed_ref, rows)

    def found_in(slots, edges):
        slots = jnp.concatenate([slots] * (edges.shape[1] // LANES), axis=1)
        return [(slots == edges[at : at + 1]).astype(f32) for at in (4, 5)]

    embed = small_ref[small_ref.shape[0] - 1][:64].astype(f32).T.astype(bf16)

    def first_terms(edges):
        units, length, harm = geometry(edges[0:1], edges[1:2], edges[2:3])
        hidden = first_hidden(length, edges[3:4], edges[7:8], embed)
        return (units, harm, hidden, contributions(hidden, small_ref[0], harm, edges[6:7]))

    edges = jnp.concatenate(tiles + [incoming], axis=1)
    units, harm, hidden, terms = first_terms(edges)
    alive = edges[6:7]
    found = found_in(slots, edges)
    pool_ref[...] = scatter(terms, incidence(*found))
    own = 2 * LANES
    geo_ref[...] = jnp.concatenate(
        [value[:, :own] for value in harm + list(units) + [alive]] + [jnp.zeros((3, own), f32)],
        axis=0,
    )

    def start_in(tile, carry):
        pool_in_ref[tile] = scatter(terms, incidence(*found_in(slots_ref[tile], edges)))
        return carry

    lax.fori_loop(1, tiles_in, start_in, 0)

    def add_edges(edges):
        _, _, _, terms = first_terms(edges)
        pool_ref[...] += scatter(terms, incidence(*found_in(slots, edges)))

        def add_in(tile, carry):
            pool_in_ref[tile] += scatter(terms, incidence(*found_in(slots_ref[tile], edges)))
            return carry

        lax.fori_loop(1, tiles_in, add_in, 0)

    def add_tile(tile, carry):
        add_edges(packed_in_ref[tile])
        return carry

    def add_block(block, carry):
        add_edges(jnp.concatenate([packed_ref[4 * block + i] for i in range(4)], axis=1))
        return carry

    lax.fori_loop(1, tiles_in, add_tile, 0)
    lax.fori_loop(0, lax.shift_right_logical(count + 511, 9), add_block, 0)

    slot = iota(found[0].shape, 0)
    edge = iota(found[0].shape, 1)
    at_slot = slot < 2 * ATOMS
    at_centre = jnp.where(
        edge < own,
        jnp.where(at_slot, found[0], 0.0),
        (slot - 2 * ATOMS == edge - own).astype(f32),
    )
    sums = incidence(at_centre, jnp.where(at_slot, found[1], 0.0))
    size = hidden.shape[0]
    ahead = dot3(top_ref[0][:, :size], rest_ref[0][:, :size], hidden)
    weight = (top_ref[0][:, size:], rest_ref[0][:, size:])
    hidden = refined(hidden, ahead, pool_ref[...], harm, sums, *weight)
    hidden_ref[...] = hidden[:, :own]
    terms = contributions(hidden, small_ref[1], harm, alive)
    env_ref[...] = scatter(terms, incidence(*[end[:ATOMS] for end in found]))
    own_top, own_rest = split(pool_ref[:ATOMS])
    first = ((0,), (0,))
    middle = 64 * even_count

    def second_in(tile, carry):
        edges = packed_in_ref[tile]
        _, harm, hidden, _ = first_terms(edges)
        at_other = (slots[:ATOMS] == edges[5:6]).astype(f32).astype(bf16)
        other = mm(own_top, at_other, first) + mm(own_rest, at_other, first)
        centre = pool_in_ref[tile].T
        even, odd = (centre[:middle] + other[:middle], centre[middle:] - other[middle:])
        scalars = jnp.concatenate([hidden, env_scalars(even, odd, harm)], axis=0)
        hidden = hidden + silu(dot3(top_ref[0], rest_ref[0], scalars))
        terms = contributions(hidden, small_ref[1], harm, 1.0)
        env_ref[...] += scatter(terms, (at_other, -at_other))
        return carry

    lax.fori_loop(1, tiles_in, second_in, 0)
    sends = send_columns(static[1:2])
    top, rest = split(env_ref[...])
    store_sides(mm(sends, top, first) + mm(sends, rest, first), up_ref, mid_ref, down_ref)


def ahead_kernel(
    hidden_ref,
    weight_top_ref,
    weight_rest_ref,
    out_hbm_ref,
    ahead_ref,
    out_top_ref,
    out_rest_ref,
    out_ref,
    semaphores,
):
    (out_copy,) = fetch([out_hbm_ref], [out_ref], semaphores)
    size = hidden_ref.shape[0]
    weight = (weight_top_ref[1][:, :size], weight_rest_ref[1][:, :size])
    ahead_ref[...] = dot3(*weight, hidden_ref[...])
    out_copy.wait()
    out_top_ref[...], out_rest_ref[...] = split(out_ref[...])


def last_kernel(
    static_ref,
    hidden_in_ref,
    ahead_ref,
    geo_ref,
    env_ref,
    before_ref,
    after_ref,
    from_up_ref,
    from_down_ref,
    weight_top_ref,
    weight_rest_ref,
    out_top_ref,
    out_rest_ref,
    small_ref,
    totals_ref,
    pool,
):
    pool[:ATOMS, :] = env_ref[...]
    load_sides(pool, ATOMS, before_ref, after_ref, from_up_ref, from_down_ref)
    at_centre, at_other = onehots(static_ref[...])
    sums = incidence(at_centre, at_other)
    harm = [geo_ref[m : m + 1] for m in range(9)]
    hidden = hidden_in_ref[...]
    size = hidden.shape[0]
    weight = (weight_top_ref[1][:, size:], weight_rest_ref[1][:, size:])
    hidden = refined(hidden, ahead_ref[...], pool[...], harm, sums, *weight)
    latent = silu(dot3(out_top_ref[...], out_rest_ref[...], hidden))
    heads = dot_stacked(small_ref[small_ref.shape[0] - 1][64:80], 2, latent)
    alive = geo_ref[12:13]
    energy = 0.5 * heads[0:1] * alive
    push = heads[1:2] * alive
    shares = jnp.concatenate(
        [energy] + [push * geo_ref[9 + i : 10 + i] for i in range(3)] + [jnp.zeros((4, energy.shape[1]), f32)],
        axis=0,
    )
    plus, minus = sums
    last = ((1,), (1,))
    part = iota((8, LANES), 1) // ATOMS == iota((8, LANES), 0)
    rows = []
    for row in range(2):
        at = slice(row * ATOMS, (row + 1) * ATOMS)
        tiled = jnp.concatenate([plus[at], minus[at], minus[at], minus[at]], axis=0)
        spread = jnp.where(part, exact(shares, tiled, last), 0.0)
        rows.append(jnp.sum(spread, axis=0, keepdims=True))
    totals_ref[...] = jnp.broadcast_to(jnp.concatenate(rows, axis=0)[None], totals_ref.shape)


def finish_kernel(layout, gathered_ref, static_ref, energy_ref, forces_ref):
    (at_x, at_y), _ = layout.position()
    own = gathered_ref[layout.at_work(at_x, at_y)][0:1]
    rows = [
        gathered_ref[layout.at_work(at_x + offset_x[k], at_y + offset_y[k])][1:2] for k in range(8)
    ]
    ghosts = pick_rows(jnp.concatenate(rows, axis=0))
    place = iota((LANES, LANES), 1)
    sends = static_ref[1:2].astype(jnp.int32)
    target = iota((LANES, LANES), 0) == place // ATOMS * ATOMS + sends
    ghosts = jnp.concatenate([ghosts] * 8, axis=0)
    total = own + exact(ghosts, target.astype(bf16), ((1,), (1,)))[0:1]
    energy_ref[...] = total[:, :ATOMS]
    for i in range(3):
        forces_ref[i : i + 1, :] = total[:, (i + 1) * ATOMS : (i + 2) * ATOMS]


def call(kernel, outs, scratch, *operands, far=(), limit=16, work=0):
    spaces = [pltpu.HBM if i in far else pltpu.VMEM for i in range(len(operands))]
    return pl.pallas_call(
        kernel,
        out_shape=[out if hasattr(out, "dtype") else jax.ShapeDtypeStruct(out, f32) for out in outs],
        in_specs=[pl.BlockSpec(memory_space=space) for space in spaces],
        out_specs=[pl.BlockSpec(memory_space=pltpu.VMEM) for _ in outs],
        scratch_shapes=scratch,
        cost_estimate=pl.CostEstimate(flops=work << 28, bytes_accessed=1 << 20, transcendentals=0)
        if work
        else None,
        compiler_params=pltpu.CompilerParams(vmem_limit_bytes=limit * 1024 * 1024),
    )(*operands)


def fetched(operands):
    buffers = [pltpu.VMEM(value.shape, value.dtype) for value in operands]
    return buffers + [pltpu.SemaphoreType.DMA((len(operands),))]


def to_all(copies):
    return lax.all_to_all(copies, ("gx", "gy"), 0, 0, tiled=True)


def exchange(layout, sides, step):
    up, mid, down = sides
    axes = ("gx", "gy")
    up = lax.ppermute(up, axes, layout.shift(step, 0))
    down = lax.ppermute(down, axes, layout.shift(-step, 0))
    to_before = jnp.stack([up[0], mid[0], down[0]])
    to_after = jnp.stack([up[2], mid[1], down[2]])
    before = lax.ppermute(to_before, axes, layout.shift(0, step))
    after = lax.ppermute(to_after, axes, layout.shift(0, -step))
    return (before, after, up, down)


def local(
    layout,
    positions,
    species,
    atom_count,
    send_list,
    edges,
    centre_embed,
    neighbour_embed,
    radial_weight,
    env_weight,
    latent_weight,
    out_weight,
    head_weight,
):
    count_edges = edges.shape[2]
    features = out_weight.shape[0]
    rows = 9 * env_weight.shape[1]
    statics = [
        atom_count[None],
        positions,
        species[None],
        jnp.transpose(send_list[0]),
        edges[0],
    ]
    (copies,) = call(
        static_kernel,
        [(layout.count, 8, LANES)],
        fetched(statics),
        *statics,
        far=range(5),
        limit=60,
    )
    layers, channels = env_weight.shape[:2]

    def half(*shape):
        return jax.ShapeDtypeStruct(shape, bf16)

    weights = [
        jnp.transpose(latent_weight, (0, 2, 1)),
        env_weight,
        radial_weight.T,
        centre_embed.T,
        neighbour_embed.T,
        head_weight,
    ]
    latent_top, latent_rest, small = call(
        weights_kernel,
        [half(*latent_weight.shape)] * 2 + [half(layers + 1, 2 * channels, features)],
        fetched(weights),
        *weights,
        far=range(6),
        limit=44,
    )
    gathered = to_all(copies)
    sides = [(ATOMS, rows), (3, 4, rows), (2, 4, rows), (3, 4, rows)]
    geo_shape = (16, count_edges)
    hidden_shape = (features, count_edges)
    domains = len(near_domains(layout, 2))
    rows_in = 2 * len(near_domains(layout, 1)) - 2
    padded = -(-(2 * domains - 2) // 8) * 8
    scratch = [
        pltpu.VMEM((2 * domains - 2, 8, LANES), f32),
        pltpu.VMEM((padded, LANES), f32),
        pltpu.VMEM((2 * domains + 4, 8, LANES), f32),
        pltpu.VMEM((2 * ATOMS + LANES, rows), f32),
        pltpu.VMEM((rows_in, LANES), f32),
        pltpu.VMEM((rows_in + 2, 8, LANES), f32),
        pltpu.VMEM((rows_in, LANES, LANES), f32),
        pltpu.VMEM((rows_in, LANES, rows), f32),
    ]
    hidden, geo, mine, home, env, *out = call(
        functools.partial(front_kernel, layout),
        [hidden_shape, geo_shape, (8, LANES), (8, LANES)] + sides,
        scratch,
        gathered,
        small,
        latent_top,
        latent_rest,
        limit=44,
    )
    ahead, out_top, out_rest = call(
        ahead_kernel,
        [hidden_shape] + [half(*out_weight.shape)] * 2,
        fetched([out_weight]),
        hidden,
        latent_top,
        latent_rest,
        out_weight,
        far=(3,),
        work=3,
    )
    ghosts = exchange(layout, out, -1)
    pool = [pltpu.VMEM((2 * ATOMS, rows), f32)]
    (totals,) = call(
        last_kernel,
        [(layout.count, 2, LANES)],
        pool,
        mine,
        hidden,
        ahead,
        geo,
        env,
        *ghosts,
        latent_top,
        latent_rest,
        out_top,
        out_rest,
        small,
    )
    totals = to_all(totals)
    energy, forces = call(
        functools.partial(finish_kernel, layout),
        [(1, ATOMS), (3, ATOMS)],
        [],
        totals,
        home,
    )
    return (energy.reshape(-1), forces)


def solution(mesh):
    layout = Layout(mesh.shape["gx"], mesh.shape["gy"])
    placed = (
        P(None, ("gx", "gy")),
        P(("gx", "gy")),
        P(("gx", "gy")),
        P(("gx", "gy"), None, None),
        P(("gx", "gy"), None, None),
        P(),
        P(),
        P(),
        P(),
        P(),
        P(),
        P(),
    )
    return jax.shard_map(
        functools.partial(local, layout),
        mesh=mesh,
        in_specs=placed,
        out_specs=(P(("gx", "gy")), P(None, ("gx", "gy"))),
        check_vma=False,
    )
```

time: 139 us -> 51.2 us (0.37)
  starting transfers between devices: 41.1 us -> 10.1 us
  local copies, waits for them, and re-layouts: 35.5 us -> 5.61 us
  waiting for transfers between devices: 28.5 us -> 5.89 us
  other arithmetic: 21.5 us -> 0.02 us
  Pallas kernels: 0 us -> 16.2 us
  blocking collectives: 0 us -> 11.4 us
  matrix products: 8.4 us -> 0 us
    ppermute x24 -> x4, starting transfers between devices: 41.1 us -> 2.68 us  [the longest x1 1.37 us: exchange(): down = lax.ppermute(down, axes, layout.shift(-step, 0))]
    ppermute x24 -> x4, waiting for transfers between devices: 28.5 us -> 4.54 us  [the longest x1 1.86 us: exchange(): up = lax.ppermute(up, axes, layout.shift(step, 0))]
    pallas_call x0 -> x6, Pallas kernels: none -> 16.2 us  [call(): pl.pallas_call(kernel, out_shape=[out if hasattr(out, 'dtype') else jax.S...]
    scatter-add x9 -> x0, other arithmetic: 15 us -> none  [the longest x4 9.15 us: local(): partial_value.at[:, centre].add(contrib).at[:, other]]
    gather x16 -> x0, local copies, waits for them, and re-layouts: 14.3 us -> none  [the longest x4 6.51 us: local(): env_centre = env_pool[:, centre].reshape(channels, 9, count_edges)]
    all_to_all x0 -> x1, blocking collectives: none -> 11.4 us  [to_all(): return lax.all_to_all(copies, ('gx', 'gy'), 0, 0, tiled=True)]
    reshape x20 -> x0, local copies, waits for them, and re-layouts: 9.24 us -> none  [the longest x4 5.41 us: local(): env_centre = env_pool[:, centre].reshape(channels, 9, count_edges)]
    dot_general x9 -> x0, matrix products: 8.4 us -> none  [the longest x2 3.08 us: refine(): return hidden + jax.nn.silu(jnp.dot(weight, scalars, precision=highest))]
  transfers between devices with their start and end apart: 24 -> 5, of which waited for: 15 -> 5; matrix products, arithmetic and copies ran while one was open for 1% -> 0% of each run, Pallas kernels for 0% -> 4%
where the time goes in v1:
time: 51.2 us; the launch traced here: 50.6 us
  Pallas kernels  16.2 us (32%)
  blocking collectives  11.4 us (22%)
  starting transfers between devices  10.1 us (20%)
  waiting for transfers between devices  5.89 us (12%)
  local copies, waits for them, and re-layouts  5.61 us (11%)
  between operations  1.36 us (3%)
    pallas_call x6, Pallas kernels, call(): pl.pallas_call(kernel, out_shape=[out if hasattr(out, 'dtype') else jax.S...  16.2 us
    all_to_all x1, blocking collectives, to_all(): return lax.all_to_all(copies, ('gx', 'gy'), 0, 0, tiled=True)  11.4 us
    all_to_all x1, starting transfers between devices, to_all(): return lax.all_to_all(copies, ('gx', 'gy'), 0, 0, tiled=True)  7.43 us
    unnamed x14, local copies, waits for them, and re-layouts  5.6 us
    ppermute x1, waiting for transfers between devices, exchange(): up = lax.ppermute(up, axes, layout.shift(step, 0))  1.86 us
    ppermute x1, waiting for transfers between devices, exchange(): after = lax.ppermute(to_after, axes, layout.shift(0, -step))  1.82 us
    ppermute x1, starting transfers between devices, exchange(): down = lax.ppermute(down, axes, layout.shift(-step, 0))  1.37 us
    all_to_all x1, waiting for transfers between devices, to_all(): return lax.all_to_all(copies, ('gx', 'gy'), 0, 0, tiled=True)  1.35 us
  transfers between devices with their start and end apart: 5, of which 5 were waited for; matrix products, arithmetic and copies ran while one was open for 0% of the time, Pallas kernels for 4%

profile of v1, /device:TPU:0, one launch (start us, length us, event | category | flops | bytes accessed | tf_op | source)
XLA Modules:
  0.0 50.6 jit_solution(2582162105281051276)
XLA Ops:
  1.3 1.6 %shard_map.131 = f32[32,8,128]{2,1,0:T(8,128)} custom-call(s32[1,1]{1,0:T(1,128)} %bitcast.11.refs_0_, f32[3,32]{1,0:T(4,128)} %refs_1_.2, s32[1,32]{1,0:T(1,128)} %bitcast.18, s32[4,8]{1,0:T(4,128)} %bitcast.16, s32[2,256]{1,0:T(2,128)} %bitcast.17), custom_call_target="tpu_custom_call" | custom-call | tf_op jit(solution)/shard_map/pallas_call | solution.py:652
  2.9 7.4 %all-to-all-start = ((f32[32,8,128]{2,1,0:T(8,128)}), f32[32,8,128]{2,1,0:T(8,128)}, u32[]{:S(2)}, u32[]{:S(2)}) async-start(f32[32,8,128]{2,1,0:T(8,128)} %shard_map.131), calls=%async_computation | async-start | bytes 262144 | tf_op jit(solution)/shard_map/all_to_all | solution.py:671
  10.3 0.0 copy-start
  10.3 1.8 %copy-done = f32[2,512,704]{1,2,0:T(8,128)S(1)} copy-done((f32[2,512,704]{1,2,0:T(8,128)S(1)}, f32[2,512,704]{1,2,0:T(8,128)}, u32[]{:S(2)}) %copy-start) | copy-done | bytes 2883608
  12.1 0.0 copy-start.2
  12.1 0.9 %copy-done.2 = f32[2,64,512]{2,1,0:T(8,128)S(1)} copy-done((f32[2,64,512]{2,1,0:T(8,128)S(1)}, f32[2,64,512]{2,1,0:T(8,128)}, u32[]{:S(2)}) %copy-start.2) | copy-done | bytes 262168
  13.1 0.0 copy-start.3
  13.1 0.7 %copy-done.3 = f32[512,8]{0,1:T(8,128)S(1)} copy-done((f32[512,8]{0,1:T(8,128)S(1)}, f32[512,8]{0,1:T(8,128)}, u32[]{:S(2)}) %copy-start.3) | copy-done | bytes 16408
  13.8 0.0 copy-start.4
  13.8 0.7 %copy-done.4 = f32[512,8]{0,1:T(8,128)S(1)} copy-done((f32[512,8]{0,1:T(8,128)S(1)}, f32[512,8]{0,1:T(8,128)}, u32[]{:S(2)}) %copy-start.4) | copy-done | bytes 16408
  14.5 0.0 copy-start.5
  14.5 0.7 %copy-done.5 = f32[512,8]{0,1:T(8,128)S(1)} copy-done((f32[512,8]{0,1:T(8,128)S(1)}, f32[512,8]{0,1:T(8,128)}, u32[]{:S(2)}) %copy-start.5) | copy-done | bytes 16408
  15.2 0.0 copy-start.6
  15.2 0.7 %copy-done.6 = f32[2,512]{1,0:T(2,128)S(1)} copy-done((f32[2,512]{1,0:T(2,128)S(1)}, f32[2,512]{1,0:T(2,128)}, u32[]{:S(2)}) %copy-start.6) | copy-done | bytes 4120
  15.9 1.2 %shard_map.132 = (bf16[2,512,704]{2,1,0:T(8,128)(2,1)S(1)}, bf16[2,512,704]{2,1,0:T(8,128)(2,1)S(1)}, bf16[3,128,512]{2,1,0:T(8,128)(2,1)S(1)}) custom-call(f32[2,704,512]{2,1,0:T(8,128)S(1)} %bitcast.12, f32[2,64,512]{2,1,0:T(8,128)S(1)} %copy-done.2, f32[8,512]{1,0:T(8,128)S(1)} %bitcast.13, f32[8,512]{1,0:T(8,128)S(1)} %bitcast.14, ...), custom_call_target="tpu_custom_call" | custom-call | tf_op jit(solution)/shard_map/pallas_call | solution.py:652
  17.2 1.3 %all-to-all-done.gathered_ref = f32[32,8,128]{2,1,0:T(8,128)} async-done(((f32[32,8,128]{2,1,0:T(8,128)}), f32[32,8,128]{2,1,0:T(8,128)}, u32[]{:S(2)}, u32[]{:S(2)}) %all-to-all-start) | async-done | bytes 131104 | tf_op jit(solution)/shard_map/all_to_all | solution.py:671
  18.5 0.0 copy-start.1
  18.5 9.7 %shard_map.133 = (f32[512,256]{1,0:T(8,128)S(1)}, f32[16,256]{1,0:T(8,128)S(1)}, f32[8,128]{1,0:T(8,128)S(1)}, f32[8,128]{1,0:T(8,128)S(1)}, f32[32,576]{1,0:T(8...) custom-call(f32[32,8,128]{2,1,0:T(8,128)} %all-to-all-done.gathered_ref, ...), custom_call_target="tpu_custom_call" | custom-call | tf_op jit(solution)/shard_map/pallas_call | solution.py:652
  28.2 0.7 %collective-permute-start = (f32[3,4,576]{2,1,0:T(4,128)S(1)}, f32[3,4,576]{2,1,0:T(4,128)S(1)}, u32[]{:S(2)}, u32[]{:S(2)}) collective-permute-start(f32[3,4,576]{2,1,0:T(4,128)S(1)} %get-tuple-element.26), channel_id=1, source_target_pairs={{0,4},{1,5},{2,6},{3,7},{8,0},{9,1},{10,2},{11,3},{16,8},{17,9},{1... | collective-permute-start | bytes 82952 | tf_op jit(solution)/shard_map/ppermute | solution.py:677
  28.9 1.4 %collective-permute-start.1 = (f32[3,4,576]{2,1,0:T(4,128)S(1)}, f32[3,4,576]{2,1,0:T(4,128)S(1)}, u32[]{:S(2)}, u32[]{:S(2)}) collective-permute-start(f32[3,4,576]{2,1,0:T(4,128)S(1)} %get-tuple-element.28), channel_id=1, source_target_pairs={{0,8},{1,9},{2,10},{3,11},{8,16},{9,17},{10,18},{11,19},{16,24},{1... | collective-permute-start | bytes 82952 | tf_op jit(solution)/shard_map/ppermute | solution.py:678
  30.3 1.9 %collective-permute-done.from_up_ref = f32[3,4,576]{2,1,0:T(4,128)S(1)} collective-permute-done((f32[3,4,576]{2,1,0:T(4,128)S(1)}, f32[3,4,576]{2,1,0:T(4,128)S(1)}, u32[]{:S(2)}, u32[]{:S(2)}) %collective-permute-start) | collective-permute-done | bytes 27680 | tf_op jit(solution)/shard_map/ppermute | solution.py:677
  32.1 0.7 %collective-permute-done.1.from_down_ref = f32[3,4,576]{2,1,0:T(4,128)S(1)} collective-permute-done((f32[3,4,576]{2,1,0:T(4,128)S(1)}, f32[3,4,576]{2,1,0:T(4,128)S(1)}, u32[]{:S(2)}, u32[]{:S(2)}) %collective-permute-start.1) | collective-permute-done | bytes 27680 | tf_op jit(solution)/shard_map/ppermute | solution.py:678
  32.8 0.1 collective-permute-start.2
  32.9 0.5 %collective-permute-start.3 = (f32[3,4,576]{2,1,0:T(4,128)S(1)}, f32[3,4,576]{2,1,0:T(4,128)S(1)}, u32[]{:S(2)}, u32[]{:S(2)}) collective-permute-start(f32[3,4,576]{2,1,0:T(4,128)S(1)} %pad_maximum_fusion.1), channel_id=1, source_target_pairs={{0,1},{1,2},{2,3},{3,0},{8,9},{9,10},{10,11},{11,8},{16,17},{17,18... | collective-permute-start | bytes 82952 | tf_op jit(solution)/shard_map/ppermute | solution.py:682
  33.4 0.0 copy-done.1
  33.4 0.8 %shard_map.134 = (f32[512,256]{1,0:T(8,128)S(1)}, bf16[512,512]{1,0:T(8,128)(2,1)S(1)}, bf16[512,512]{1,0:T(8,128)(2,1)S(1)}) custom-call(f32[512,256]{1,0:T(8,128)S(1)} %get-tuple-element.22.hidden_ref.hidden_in_ref, bf16[2,512,704]{2,1,0:T(8,128)(2,1)S(1)} %get-tuple-element.19.top_ref.weight_top_ref, ...), custom_call_target="tpu_custom_call" | custom-call | flops 805306368 | bytes 1048576 | tf_op jit(solution)/shard_map/pallas_call | solution.py:652
  34.2 0.2 collective-permute-done.2.before_ref
  34.4 1.8 %collective-permute-done.3.after_ref = f32[3,4,576]{2,1,0:T(4,128)S(1)} collective-permute-done((f32[3,4,576]{2,1,0:T(4,128)S(1)}, f32[3,4,576]{2,1,0:T(4,128)S(1)}, u32[]{:S(2)}, u32[]{:S(2)}) %collective-permute-start.3) | collective-permute-done | bytes 27680 | tf_op jit(solution)/shard_map/ppermute | solution.py:682
  36.3 2.1 %shard_map.135 = f32[32,2,128]{2,1,0:T(2,128)S(1)} custom-call(f32[8,128]{1,0:T(8,128)S(1)} %get-tuple-element.21.static_ref, f32[512,256]{1,0:T(8,128)S(1)} %get-tuple-element.22.hidden_ref.hidden_in_ref, f32[512,256]{1,0:T(8,128)S(1)} %get-tuple-element.23.ahead_ref, f32[16,256]{1,0:T(8,128)S(1)} %get-tuple-element.24.geo_ref, ...), custom_call_target="tpu_custom_call" | custom-call | tf_op jit(solution)/shard_map/pallas_call | solution.py:652
  38.4 11.4 %all_to_all.10.gathered_ref = f32[32,2,128]{2,1,0:T(2,128)S(1)} all-to-all(f32[32,2,128]{2,1,0:T(2,128)S(1)} %shard_map.135), channel_id=1, replica_groups=mesh['gx'=8,'gy'=4] {'gx','gy'}, dimensions={0} | all-to-all | bytes 65536 | tf_op jit(solution)/shard_map/all_to_all | solution.py:671
  49.8 0.8 %shard_map.136 = (f32[1,32]{1,0:T(1,128)}, f32[3,32]{1,0:T(4,128)}) custom-call(f32[32,2,128]{2,1,0:T(2,128)S(1)} %all_to_all.10.gathered_ref, f32[8,128]{1,0:T(8,128)S(1)} %get-tuple-element.31.static_ref), custom_call_target="tpu_custom_call" | custom-call | tf_op jit(solution)/shard_map/pallas_call | solution.py:652
  (5 shorter events, 0.0 us)
Async XLA Ops:
  2.9 15.6 %all-to-all-start = ((f32[32,8,128]{2,1,0:T(8,128)}), f32[32,8,128]{2,1,0:T(8,128)}, u32[]{:S(2)}, u32[]{:S(2)}) async-start(f32[32,8,128]{2,1,0:T(8,128)} %shard_map.131), calls=%async_computation | async-start | bytes 262144 | tf_op jit(solution)/shard_map/all_to_all | solution.py:671
  10.3 1.8 %copy-start = (f32[2,512,704]{1,2,0:T(8,128)S(1)}, f32[2,512,704]{1,2,0:T(8,128)}, u32[]{:S(2)}) copy-start(f32[2,512,704]{1,2,0:T(8,128)} %param.21) | copy-start | bytes 8650756
  12.1 0.9 %copy-start.2 = (f32[2,64,512]{2,1,0:T(8,128)S(1)}, f32[2,64,512]{2,1,0:T(8,128)}, u32[]{:S(2)}) copy-start(f32[2,64,512]{2,1,0:T(8,128)} %refs_1_.3) | copy-start | bytes 786436
  13.1 0.7 %copy-start.3 = (f32[512,8]{0,1:T(8,128)S(1)}, f32[512,8]{0,1:T(8,128)}, u32[]{:S(2)}) copy-start(f32[512,8]{0,1:T(8,128)} %param.19) | copy-start | bytes 49156
  13.8 0.7 %copy-start.4 = (f32[512,8]{0,1:T(8,128)S(1)}, f32[512,8]{0,1:T(8,128)}, u32[]{:S(2)}) copy-start(f32[512,8]{0,1:T(8,128)} %param.17) | copy-start | bytes 49156
  14.5 0.7 %copy-start.5 = (f32[512,8]{0,1:T(8,128)S(1)}, f32[512,8]{0,1:T(8,128)}, u32[]{:S(2)}) copy-start(f32[512,8]{0,1:T(8,128)} %param.18) | copy-start | bytes 49156
  15.2 0.7 %copy-start.6 = (f32[2,512]{1,0:T(2,128)S(1)}, f32[2,512]{1,0:T(2,128)}, u32[]{:S(2)}) copy-start(f32[2,512]{1,0:T(2,128)} %refs_5_.1) | copy-start | bytes 12292
  18.5 14.9 %copy-start.1 = (f32[512,512]{1,0:T(8,128)S(1)}, f32[512,512]{1,0:T(8,128)}, u32[]{:S(2)}) copy-start(f32[512,512]{1,0:T(8,128)} %out_hbm_ref.1) | copy-start | bytes 3145732
  28.2 3.9 %collective-permute-start = (f32[3,4,576]{2,1,0:T(4,128)S(1)}, f32[3,4,576]{2,1,0:T(4,128)S(1)}, u32[]{:S(2)}, u32[]{:S(2)}) collective-permute-start(f32[3,4,576]{2,1,0:T(4,128)S(1)} %get-tuple-element.26), channel_id=1, source_target_pairs={{0,4},{1,5},{2,6},{3,7},{8,0},{9,1},{10,2},{11,3},{16,8},{17,9},{1... | collective-permute-start | bytes 82952 | tf_op jit(solution)/shard_map/ppermute | solution.py:677
  28.9 3.9 %collective-permute-start.1 = (f32[3,4,576]{2,1,0:T(4,128)S(1)}, f32[3,4,576]{2,1,0:T(4,128)S(1)}, u32[]{:S(2)}, u32[]{:S(2)}) collective-permute-start(f32[3,4,576]{2,1,0:T(4,128)S(1)} %get-tuple-element.28), channel_id=1, source_target_pairs={{0,8},{1,9},{2,10},{3,11},{8,16},{9,17},{10,18},{11,19},{16,24},{1... | collective-permute-start | bytes 82952 | tf_op jit(solution)/shard_map/ppermute | solution.py:678
  32.8 1.6 %collective-permute-start.2 = (f32[3,4,576]{2,1,0:T(4,128)S(1)}, f32[3,4,576]{2,1,0:T(4,128)S(1)}, u32[]{:S(2)}, u32[]{:S(2)}) collective-permute-start(f32[3,4,576]{2,1,0:T(4,128)S(1)} %pad_maximum_fusion), channel_id=1, source_target_pairs={{0,3},{1,0},{2,1},{3,2},{8,11},{9,8},{10,9},{11,10},{16,19},{17,16... | collective-permute-start | bytes 82952 | tf_op jit(solution)/shard_map/ppermute | solution.py:681
  32.9 3.4 %collective-permute-start.3 = (f32[3,4,576]{2,1,0:T(4,128)S(1)}, f32[3,4,576]{2,1,0:T(4,128)S(1)}, u32[]{:S(2)}, u32[]{:S(2)}) collective-permute-start(f32[3,4,576]{2,1,0:T(4,128)S(1)} %pad_maximum_fusion.1), channel_id=1, source_target_pairs={{0,1},{1,2},{2,3},{3,0},{8,9},{9,10},{10,11},{11,8},{16,17},{17,18... | collective-permute-start | bytes 82952 | tf_op jit(solution)/shard_map/ppermute | solution.py:682

commit v2 on v1

--- a/solution.py
+++ b/solution.py
@@ -226,28 +226,32 @@
 
 
 def weights_kernel(*refs):
-    sources, outs, targets, semaphores = (refs[:6], refs[6:9], refs[9:15], refs[15])
+    sources, outs, targets, semaphores = (refs[:2], refs[2:5], refs[5:7], refs[7])
     latent_top_ref, latent_rest_ref, small_ref = outs
-    latent_ref, env_ref, radial_ref, centre_ref, neighbour_ref, head_ref = targets
+    latent_ref, joined_ref = targets
+    layers, twice = (latent_ref.shape[0], small_ref.shape[1])
+    channels = twice // 2
     for copy in fetch(sources, targets, semaphores):
         copy.wait()
     for layer in range(latent_ref.shape[0]):
         top, rest = split(latent_ref[layer].T)
         latent_top_ref[layer] = top
         latent_rest_ref[layer] = rest
-        top, rest = split(env_ref[layer])
+        at = 24 + layer * channels
+        top, rest = split(joined_ref[at : at + channels, :])
         small_ref[layer] = jnp.concatenate([top, rest], axis=0)
 
     def halves(value):
         top = value.astype(bf16).astype(f32)
         return (top, value - top)
 
-    radial, centre, neighbour = (halves(r[...]) for r in (radial_ref, centre_ref, neighbour_ref))
+    embeds = [joined_ref[8 * i : 8 * i + 8, :] for i in range(3)]
+    radial, centre, neighbour = (halves(value) for value in embeds)
     stacked = [radial[0], radial[0], radial[1], centre[0], neighbour[0], centre[1], neighbour[1]]
-    top, rest = halves(head_ref[...])
+    top, rest = halves(joined_ref[24 + layers * channels :, :])
     zeros = jnp.zeros((60, top.shape[1]), f32)
     stacked = stacked + [jnp.zeros_like(radial[0]), top, rest, zeros]
-    small_ref[env_ref.shape[0]] = jnp.concatenate(stacked, axis=0).astype(bf16)
+    small_ref[layers] = jnp.concatenate(stacked, axis=0).astype(bf16)
 
 
 def lane_pick(rows, index):
@@ -434,9 +438,11 @@
     named = jnp.max(jnp.maximum(*named), axis=1, keepdims=True) > 0
     slots = jnp.concatenate([slots[:ATOMS], jnp.where(named, slots[ATOMS:], -1.0)], axis=0)
 
-    def touches(slots, tile):
-        found = jnp.where((slots == tile[4:5]) | (slots == tile[5:6]), 1.0, 0.0)
-        return jnp.max(found, axis=0, keepdims=True)
+    def touches(slots, tile, nearest):
+        found = slots == tile[5:6]
+        if nearest:
+            found = found | (slots == tile[4:5])
+        return jnp.max(jnp.where(found, 1.0, 0.0), axis=0, keepdims=True)
 
     chosen_ref[...] = jnp.zeros_like(chosen_ref)
     domains = near_domains(layout, 2)
@@ -462,7 +468,8 @@
             tile = rows_ref[at]
             live = tile[6:7] - coming_ref[at : at + 1, :] if at < rows_in else tile[6:7]
             row = slice(at, at + 1)
-            chosen_ref[row, :] = jnp.maximum(chosen_ref[row, :], touches(slots, tile) * live)
+            found = touches(slots, tile, at < rows_in) * live
+            chosen_ref[row, :] = jnp.maximum(chosen_ref[row, :], found)
 
     choose(slots)
 
@@ -721,20 +728,15 @@
     def half(*shape):
         return jax.ShapeDtypeStruct(shape, bf16)
 
-    weights = [
-        jnp.transpose(latent_weight, (0, 2, 1)),
-        env_weight,
-        radial_weight.T,
-        centre_embed.T,
-        neighbour_embed.T,
-        head_weight,
-    ]
+    joined = [radial_weight.T, centre_embed.T, neighbour_embed.T]
+    joined += [env_weight.reshape(layers * channels, features), head_weight]
+    weights = [jnp.transpose(latent_weight, (0, 2, 1)), jnp.concatenate(joined, axis=0)]
     latent_top, latent_rest, small = call(
         weights_kernel,
         [half(*latent_weight.shape)] * 2 + [half(layers + 1, 2 * channels, features)],
         fetched(weights),
         *weights,
-        far=range(6),
+        far=range(2),
         limit=44,
     )
     gathered = to_all(copies)

time: 51.2 us -> 51.2 us (level)
    concatenate x0 -> x1, local copies, waits for them, and re-layouts: none -> 0.7 us  [local(): jnp.concatenate(joined, axis=0)]
    unnamed x14 -> x8, local copies, waits for them, and re-layouts: 5.6 us -> 4.94 us
  transfers between devices with their start and end apart: 5 -> 5, of which waited for: 5 -> 5; matrix products, arithmetic and copies ran while one was open for 0% -> 8% of each run, Pallas kernels for 4% -> 4%
where the time goes in v2:
time: 51.2 us; the launch traced here: 50.6 us
  Pallas kernels  16.2 us (32%)
  blocking collectives  11 us (21%)
  starting transfers between devices  10.1 us (20%)
  waiting for transfers between devices  6.32 us (12%)
  local copies, waits for them, and re-layouts  5.65 us (11%)
  between operations  1.36 us (3%)
    pallas_call x6, Pallas kernels, call(): pl.pallas_call(kernel, out_shape=[out if hasattr(out, 'dtype') else jax.S...  16.2 us
    all_to_all x1, blocking collectives, to_all(): return lax.all_to_all(copies, ('gx', 'gy'), 0, 0, tiled=True)  11 us
    all_to_all x1, starting transfers between devices, to_all(): return lax.all_to_all(copies, ('gx', 'gy'), 0, 0, tiled=True)  7.43 us
    unnamed x8, local copies, waits for them, and re-layouts  4.94 us
    ppermute x1, waiting for transfers between devices, exchange(): after = lax.ppermute(to_after, axes, layout.shift(0, -step))  2.07 us
    ppermute x1, waiting for transfers between devices, exchange(): up = lax.ppermute(up, axes, layout.shift(step, 0))  1.86 us
    ppermute x1, starting transfers between devices, exchange(): down = lax.ppermute(down, axes, layout.shift(-step, 0))  1.36 us
    all_to_all x1, waiting for transfers between devices, to_all(): return lax.all_to_all(copies, ('gx', 'gy'), 0, 0, tiled=True)  1.34 us
  transfers between devices with their start and end apart: 5, of which 5 were waited for; matrix products, arithmetic and copies ran while one was open for 8% of the time, Pallas kernels for 4%

profile of v2, /device:TPU:0, one launch (start us, length us, event | category | flops | bytes accessed | tf_op | source)
XLA Modules:
  0.0 50.6 jit_solution(2917940390182792164)
XLA Ops:
  1.3 1.6 %shard_map.131 = f32[32,8,128]{2,1,0:T(8,128)} custom-call(s32[1,1]{1,0:T(1,128)} %bitcast.15.refs_0_, f32[3,32]{1,0:T(4,128)} %refs_1_.1, s32[1,32]{1,0:T(1,128)} %bitcast.20, s32[4,8]{1,0:T(4,128)} %bitcast.18, s32[2,256]{1,0:T(2,128)} %bitcast.19), custom_call_target="tpu_custom_call" | custom-call | tf_op jit(solution)/shard_map/pallas_call | solution.py:659
  2.9 7.4 %all-to-all-start = ((f32[32,8,128]{2,1,0:T(8,128)}), f32[32,8,128]{2,1,0:T(8,128)}, u32[]{:S(2)}, u32[]{:S(2)}) async-start(f32[32,8,128]{2,1,0:T(8,128)} %shard_map.131), calls=%async_computation | async-start | bytes 262144 | tf_op jit(solution)/shard_map/all_to_all | solution.py:678
  10.3 0.7 %bitcast_dynamic-update-slice_fusion.2 = f32[154,512]{1,0:T(8,128)S(1)} fusion(f32[512,8]{0,1:T(8,128)} %param.19), kind=kLoop, calls=%fused_computation.4 | loop fusion | bytes 32768
  11.0 0.7 %bitcast_dynamic-update-slice_fusion.1 = f32[154,512]{1,0:T(8,128)S(1)} fusion(f32[154,512]{1,0:T(8,128)S(1)} %bitcast_dynamic-update-slice_fusion.2, f32[512,8]{0,1:T(8,128)} %param.17), kind=kLoop, calls=%fused_computation.3 | loop fusion | bytes 32768
  11.7 0.7 %bitcast_dynamic-update-slice_fusion = f32[154,512]{1,0:T(8,128)S(1)} fusion(f32[154,512]{1,0:T(8,128)S(1)} %bitcast_dynamic-update-slice_fusion.1, f32[512,8]{0,1:T(8,128)} %param.18), kind=kLoop, calls=%fused_computation.2 | loop fusion | bytes 32768
  12.5 1.0 %constant_dynamic-update-slice_fusion.1 = f32[154,512]{1,0:T(8,128)S(1)} fusion(f32[154,512]{1,0:T(8,128)S(1)} %bitcast_dynamic-update-slice_fusion, f32[128,512]{1,0:T(8,128)} %bitcast.17), kind=kLoop, calls=%fused_computation.6 | loop fusion | bytes 524288
  13.4 0.7 %constant_dynamic-update-slice_fusion.refs_1_ = f32[154,512]{1,0:T(8,128)S(1)} fusion(f32[154,512]{1,0:T(8,128)S(1)} %constant_dynamic-update-slice_fusion.1, f32[2,512]{1,0:T(2,128)} %param.23), kind=kLoop, calls=%fused_computation.5 | loop fusion | bytes 8192 | tf_op jit(solution)/shard_map/concatenate | solution.py:733
  14.1 0.0 copy-start
  14.1 1.8 %copy-done = f32[2,512,704]{1,2,0:T(8,128)S(1)} copy-done((f32[2,512,704]{1,2,0:T(8,128)S(1)}, f32[2,512,704]{1,2,0:T(8,128)}, u32[]{:S(2)}) %copy-start) | copy-done | bytes 2883608
  15.9 1.2 %shard_map.132 = (bf16[2,512,704]{2,1,0:T(8,128)(2,1)S(1)}, bf16[2,512,704]{2,1,0:T(8,128)(2,1)S(1)}, bf16[3,128,512]{2,1,0:T(8,128)(2,1)S(1)}) custom-call(f32[2,704,512]{2,1,0:T(8,128)S(1)} %bitcast.16, f32[154,512]{1,0:T(8,128)S(1)} %constant_dynamic-update-slice_fusion.refs_1_), custom_call_target="tpu_custom_call" | custom-call | tf_op jit(solution)/shard_map/pallas_call | solution.py:659
  17.2 1.3 %all-to-all-done.gathered_ref = f32[32,8,128]{2,1,0:T(8,128)} async-done(((f32[32,8,128]{2,1,0:T(8,128)}), f32[32,8,128]{2,1,0:T(8,128)}, u32[]{:S(2)}, u32[]{:S(2)}) %all-to-all-start) | async-done | bytes 131104 | tf_op jit(solution)/shard_map/all_to_all | solution.py:678
  18.5 0.0 copy-start.1
  18.5 9.7 %shard_map.133 = (f32[512,256]{1,0:T(8,128)S(1)}, f32[16,256]{1,0:T(8,128)S(1)}, f32[8,128]{1,0:T(8,128)S(1)}, f32[8,128]{1,0:T(8,128)S(1)}, f32[32,576]{1,0:T(8...) custom-call(f32[32,8,128]{2,1,0:T(8,128)} %all-to-all-done.gathered_ref, ...), custom_call_target="tpu_custom_call" | custom-call | tf_op jit(solution)/shard_map/pallas_call | solution.py:659
  28.2 0.7 %collective-permute-start = (f32[3,4,576]{2,1,0:T(4,128)S(1)}, f32[3,4,576]{2,1,0:T(4,128)S(1)}, u32[]{:S(2)}, u32[]{:S(2)}) collective-permute-start(f32[3,4,576]{2,1,0:T(4,128)S(1)} %get-tuple-element.26), channel_id=1, source_target_pairs={{0,4},{1,5},{2,6},{3,7},{8,0},{9,1},{10,2},{11,3},{16,8},{17,9},{1... | collective-permute-start | bytes 82952 | tf_op jit(solution)/shard_map/ppermute | solution.py:684
  28.9 1.4 %collective-permute-start.1 = (f32[3,4,576]{2,1,0:T(4,128)S(1)}, f32[3,4,576]{2,1,0:T(4,128)S(1)}, u32[]{:S(2)}, u32[]{:S(2)}) collective-permute-start(f32[3,4,576]{2,1,0:T(4,128)S(1)} %get-tuple-element.28), channel_id=1, source_target_pairs={{0,8},{1,9},{2,10},{3,11},{8,16},{9,17},{10,18},{11,19},{16,24},{1... | collective-permute-start | bytes 82952 | tf_op jit(solution)/shard_map/ppermute | solution.py:685
  30.3 1.9 %collective-permute-done.from_up_ref = f32[3,4,576]{2,1,0:T(4,128)S(1)} collective-permute-done((f32[3,4,576]{2,1,0:T(4,128)S(1)}, f32[3,4,576]{2,1,0:T(4,128)S(1)}, u32[]{:S(2)}, u32[]{:S(2)}) %collective-permute-start) | collective-permute-done | bytes 27680 | tf_op jit(solution)/shard_map/ppermute | solution.py:684
  32.1 0.9 %collective-permute-done.1.from_down_ref = f32[3,4,576]{2,1,0:T(4,128)S(1)} collective-permute-done((f32[3,4,576]{2,1,0:T(4,128)S(1)}, f32[3,4,576]{2,1,0:T(4,128)S(1)}, u32[]{:S(2)}, u32[]{:S(2)}) %collective-permute-start.1) | collective-permute-done | bytes 27680 | tf_op jit(solution)/shard_map/ppermute | solution.py:685
  33.0 0.1 collective-permute-start.2
  33.1 0.5 %collective-permute-start.3 = (f32[3,4,576]{2,1,0:T(4,128)S(1)}, f32[3,4,576]{2,1,0:T(4,128)S(1)}, u32[]{:S(2)}, u32[]{:S(2)}) collective-permute-start(f32[3,4,576]{2,1,0:T(4,128)S(1)} %pad_maximum_fusion.1), channel_id=1, source_target_pairs={{0,1},{1,2},{2,3},{3,0},{8,9},{9,10},{10,11},{11,8},{16,17},{17,18... | collective-permute-start | bytes 82952 | tf_op jit(solution)/shard_map/ppermute | solution.py:689
  33.6 0.0 copy-done.1
  33.6 0.8 %shard_map.134 = (f32[512,256]{1,0:T(8,128)S(1)}, bf16[512,512]{1,0:T(8,128)(2,1)S(1)}, bf16[512,512]{1,0:T(8,128)(2,1)S(1)}) custom-call(f32[512,256]{1,0:T(8,128)S(1)} %get-tuple-element.22.hidden_ref.hidden_in_ref, bf16[2,512,704]{2,1,0:T(8,128)(2,1)S(1)} %get-tuple-element.19.top_ref.weight_top_ref, ...), custom_call_target="tpu_custom_call" | custom-call | flops 805306368 | bytes 1048576 | tf_op jit(solution)/shard_map/pallas_call | solution.py:659
  34.4 0.2 collective-permute-done.2.before_ref
  34.6 2.1 %collective-permute-done.3.after_ref = f32[3,4,576]{2,1,0:T(4,128)S(1)} collective-permute-done((f32[3,4,576]{2,1,0:T(4,128)S(1)}, f32[3,4,576]{2,1,0:T(4,128)S(1)}, u32[]{:S(2)}, u32[]{:S(2)}) %collective-permute-start.3) | collective-permute-done | bytes 27680 | tf_op jit(solution)/shard_map/ppermute | solution.py:689
  36.7 2.1 %shard_map.135 = f32[32,2,128]{2,1,0:T(2,128)S(1)} custom-call(f32[8,128]{1,0:T(8,128)S(1)} %get-tuple-element.21.static_ref, f32[512,256]{1,0:T(8,128)S(1)} %get-tuple-element.22.hidden_ref.hidden_in_ref, f32[512,256]{1,0:T(8,128)S(1)} %get-tuple-element.23.ahead_ref, f32[16,256]{1,0:T(8,128)S(1)} %get-tuple-element.24.geo_ref, ...), custom_call_target="tpu_custom_call" | custom-call | tf_op jit(solution)/shard_map/pallas_call | solution.py:659
  38.8 11.0 %all_to_all.10.gathered_ref = f32[32,2,128]{2,1,0:T(2,128)S(1)} all-to-all(f32[32,2,128]{2,1,0:T(2,128)S(1)} %shard_map.135), channel_id=1, replica_groups=mesh['gx'=8,'gy'=4] {'gx','gy'}, dimensions={0} | all-to-all | bytes 65536 | tf_op jit(solution)/shard_map/all_to_all | solution.py:678
  49.8 0.8 %shard_map.136 = (f32[1,32]{1,0:T(1,128)}, f32[3,32]{1,0:T(4,128)}) custom-call(f32[32,2,128]{2,1,0:T(2,128)S(1)} %all_to_all.10.gathered_ref, f32[8,128]{1,0:T(8,128)S(1)} %get-tuple-element.31.static_ref), custom_call_target="tpu_custom_call" | custom-call | tf_op jit(solution)/shard_map/pallas_call | solution.py:659
  (5 shorter events, 0.0 us)
Async XLA Ops:
  2.9 15.6 %all-to-all-start = ((f32[32,8,128]{2,1,0:T(8,128)}), f32[32,8,128]{2,1,0:T(8,128)}, u32[]{:S(2)}, u32[]{:S(2)}) async-start(f32[32,8,128]{2,1,0:T(8,128)} %shard_map.131), calls=%async_computation | async-start | bytes 262144 | tf_op jit(solution)/shard_map/all_to_all | solution.py:678
  14.1 1.8 %copy-start = (f32[2,512,704]{1,2,0:T(8,128)S(1)}, f32[2,512,704]{1,2,0:T(8,128)}, u32[]{:S(2)}) copy-start(f32[2,512,704]{1,2,0:T(8,128)} %param.21) | copy-start | bytes 8650756
  18.5 15.1 %copy-start.1 = (f32[512,512]{1,0:T(8,128)S(1)}, f32[512,512]{1,0:T(8,128)}, u32[]{:S(2)}) copy-start(f32[512,512]{1,0:T(8,128)} %out_hbm_ref.1) | copy-start | bytes 3145732
  28.2 3.9 %collective-permute-start = (f32[3,4,576]{2,1,0:T(4,128)S(1)}, f32[3,4,576]{2,1,0:T(4,128)S(1)}, u32[]{:S(2)}, u32[]{:S(2)}) collective-permute-start(f32[3,4,576]{2,1,0:T(4,128)S(1)} %get-tuple-element.26), channel_id=1, source_target_pairs={{0,4},{1,5},{2,6},{3,7},{8,0},{9,1},{10,2},{11,3},{16,8},{17,9},{1... | collective-permute-start | bytes 82952 | tf_op jit(solution)/shard_map/ppermute | solution.py:684
  28.9 4.1 %collective-permute-start.1 = (f32[3,4,576]{2,1,0:T(4,128)S(1)}, f32[3,4,576]{2,1,0:T(4,128)S(1)}, u32[]{:S(2)}, u32[]{:S(2)}) collective-permute-start(f32[3,4,576]{2,1,0:T(4,128)S(1)} %get-tuple-element.28), channel_id=1, source_target_pairs={{0,8},{1,9},{2,10},{3,11},{8,16},{9,17},{10,18},{11,19},{16,24},{1... | collective-permute-start | bytes 82952 | tf_op jit(solution)/shard_map/ppermute | solution.py:685
  33.0 1.6 %collective-permute-start.2 = (f32[3,4,576]{2,1,0:T(4,128)S(1)}, f32[3,4,576]{2,1,0:T(4,128)S(1)}, u32[]{:S(2)}, u32[]{:S(2)}) collective-permute-start(f32[3,4,576]{2,1,0:T(4,128)S(1)} %pad_maximum_fusion), channel_id=1, source_target_pairs={{0,3},{1,0},{2,1},{3,2},{8,11},{9,8},{10,9},{11,10},{16,19},{17,16... | collective-permute-start | bytes 82952 | tf_op jit(solution)/shard_map/ppermute | solution.py:688
  33.1 3.6 %collective-permute-start.3 = (f32[3,4,576]{2,1,0:T(4,128)S(1)}, f32[3,4,576]{2,1,0:T(4,128)S(1)}, u32[]{:S(2)}, u32[]{:S(2)}) collective-permute-start(f32[3,4,576]{2,1,0:T(4,128)S(1)} %pad_maximum_fusion.1), channel_id=1, source_target_pairs={{0,1},{1,2},{2,3},{3,0},{8,9},{9,10},{10,11},{11,8},{16,17},{17,18... | collective-permute-start | bytes 82952 | tf_op jit(solution)/shard_map/ppermute | solution.py:689

commit v3 on v2

--- a/solution.py
+++ b/solution.py
@@ -226,17 +226,14 @@
 
 
 def weights_kernel(*refs):
-    sources, outs, targets, semaphores = (refs[:2], refs[2:5], refs[5:7], refs[7])
-    latent_top_ref, latent_rest_ref, small_ref = outs
+    sources, outs, targets, semaphores = (refs[:2], refs[2:4], refs[4:6], refs[6])
+    latent_halves_ref, small_ref = outs
     latent_ref, joined_ref = targets
-    layers, twice = (latent_ref.shape[0], small_ref.shape[1])
-    channels = twice // 2
+    layers, channels = (small_ref.shape[0] - 1, small_ref.shape[1] // 2)
     for copy in fetch(sources, targets, semaphores):
         copy.wait()
-    for layer in range(latent_ref.shape[0]):
-        top, rest = split(latent_ref[layer].T)
-        latent_top_ref[layer] = top
-        latent_rest_ref[layer] = rest
+    latent_halves_ref[0], latent_halves_ref[1] = split(latent_ref[...].T)
+    for layer in range(layers):
         at = 24 + layer * channels
         top, rest = split(joined_ref[at : at + channels, :])
         small_ref[layer] = jnp.concatenate([top, rest], axis=0)
@@ -402,8 +399,7 @@
     layout,
     gathered_ref,
     small_ref,
-    top_ref,
-    rest_ref,
+    halves_ref,
     hidden_ref,
     geo_ref,
     static_ref,
@@ -541,8 +537,8 @@
     )
     sums = incidence(at_centre, jnp.where(at_slot, found[1], 0.0))
     size = hidden.shape[0]
-    ahead = dot3(top_ref[0][:, :size], rest_ref[0][:, :size], hidden)
-    weight = (top_ref[0][:, size:], rest_ref[0][:, size:])
+    ahead = dot3(halves_ref[0][:, :size], halves_ref[1][:, :size], hidden)
+    weight = (halves_ref[0][:, size:], halves_ref[1][:, size:])
     hidden = refined(hidden, ahead, pool_ref[...], harm, sums, *weight)
     hidden_ref[...] = hidden[:, :own]
     terms = contributions(hidden, small_ref[1], harm, alive)
@@ -559,7 +555,7 @@
         centre = pool_in_ref[tile].T
         even, odd = (centre[:middle] + other[:middle], centre[middle:] - other[middle:])
         scalars = jnp.concatenate([hidden, env_scalars(even, odd, harm)], axis=0)
-        hidden = hidden + silu(dot3(top_ref[0], rest_ref[0], scalars))
+        hidden = hidden + silu(dot3(halves_ref[0], halves_ref[1], scalars))
         terms = contributions(hidden, small_ref[1], harm, 1.0)
         env_ref[...] += scatter(terms, (at_other, -at_other))
         return carry
@@ -572,19 +568,25 @@
 
 def ahead_kernel(
     hidden_ref,
-    weight_top_ref,
-    weight_rest_ref,
+    latent_hbm_ref,
     out_hbm_ref,
     ahead_ref,
+    sums_top_ref,
+    sums_rest_ref,
     out_top_ref,
     out_rest_ref,
+    latent_ref,
     out_ref,
     semaphores,
 ):
-    (out_copy,) = fetch([out_hbm_ref], [out_ref], semaphores)
+    sources = [latent_hbm_ref.at[1], out_hbm_ref]
+    latent_copy, out_copy = fetch(sources, [latent_ref, out_ref], semaphores)
+    latent_copy.wait()
     size = hidden_ref.shape[0]
-    weight = (weight_top_ref[1][:, :size], weight_rest_ref[1][:, :size])
-    ahead_ref[...] = dot3(*weight, hidden_ref[...])
+    top, rest = split(latent_ref[...].T)
+    ahead_ref[...] = dot3(top[:, :size], rest[:, :size], hidden_ref[...])
+    sums_top_ref[...] = top[:, size:]
+    sums_rest_ref[...] = rest[:, size:]
     out_copy.wait()
     out_top_ref[...], out_rest_ref[...] = split(out_ref[...])
 
@@ -613,8 +615,7 @@
     sums = incidence(at_centre, at_other)
     harm = [geo_ref[m : m + 1] for m in range(9)]
     hidden = hidden_in_ref[...]
-    size = hidden.shape[0]
-    weight = (weight_top_ref[1][:, size:], weight_rest_ref[1][:, size:])
+    weight = (weight_top_ref[...], weight_rest_ref[...])
     hidden = refined(hidden, ahead_ref[...], pool[...], harm, sums, *weight)
     latent = silu(dot3(out_top_ref[...], out_rest_ref[...], hidden))
     heads = dot_stacked(small_ref[small_ref.shape[0] - 1][64:80], 2, latent)
@@ -730,10 +731,11 @@
 
     joined = [radial_weight.T, centre_embed.T, neighbour_embed.T]
     joined += [env_weight.reshape(layers * channels, features), head_weight]
-    weights = [jnp.transpose(latent_weight, (0, 2, 1)), jnp.concatenate(joined, axis=0)]
-    latent_top, latent_rest, small = call(
+    latent_turned = jnp.transpose(latent_weight, (0, 2, 1))
+    weights = [latent_turned[0], jnp.concatenate(joined, axis=0)]
+    latent_halves, small = call(
         weights_kernel,
-        [half(*latent_weight.shape)] * 2 + [half(layers + 1, 2 * channels, features)],
+        [half(2, *latent_weight.shape[1:]), half(layers + 1, 2 * channels, features)],
         fetched(weights),
         *weights,
         far=range(2),
@@ -762,19 +764,19 @@
         scratch,
         gathered,
         small,
-        latent_top,
-        latent_rest,
+        latent_halves,
         limit=44,
     )
-    ahead, out_top, out_rest = call(
+    late = [latent_turned, out_weight]
+    ahead, sums_top, sums_rest, out_top, out_rest = call(
         ahead_kernel,
-        [hidden_shape] + [half(*out_weight.shape)] * 2,
-        fetched([out_weight]),
+        [hidden_shape]
+        + [half(features, latent_weight.shape[2] - features)] * 2
+        + [half(*out_weight.shape)] * 2,
+        fetched([latent_turned[1], out_weight]),
         hidden,
-        latent_top,
-        latent_rest,
-        out_weight,
-        far=(3,),
+        *late,
+        far=(1, 2),
         work=3,
     )
     ghosts = exchange(layout, out, -1)
@@ -789,8 +791,8 @@
         geo,
         env,
         *ghosts,
-        latent_top,
-        latent_rest,
+        sums_top,
+        sums_rest,
         out_top,
         out_rest,
         small,

time: 51.2 us -> 52.3 us (1.021)
  waiting for transfers between devices: 6.32 us -> 3.98 us
  local copies, waits for them, and re-layouts: 5.65 us -> 7.89 us
  starting transfers between devices: 10.1 us -> 11.2 us
  blocking collectives: 11 us -> 12 us
  Pallas kernels: 16.2 us -> 15.3 us
    ppermute x1, waiting for transfers between devices: 2.07 us -> 0.28 us  [exchange(): after = lax.ppermute(to_after, axes, layout.shift(0, -step))]
    ppermute x1, starting transfers between devices: 0.06 us -> 1.78 us  [exchange(): before = lax.ppermute(to_before, axes, layout.shift(0, step))]
    squeeze x0 -> x1, local copies, waits for them, and re-layouts: none -> 1.47 us  [local(): weights = [latent_turned[0], jnp.concatenate(joined, axis=0)]]
    all_to_all x1, blocking collectives: 11 us -> 12 us  [to_all(): return lax.all_to_all(copies, ('gx', 'gy'), 0, 0, tiled=True)]
    pallas_call x6, Pallas kernels: 16.2 us -> 15.3 us  [call(): pl.pallas_call(kernel, out_shape=[out if hasattr(out, 'dtype') else jax.S...]
    unnamed x8 -> x12, local copies, waits for them, and re-layouts: 4.94 us -> 5.71 us
  transfers between devices with their start and end apart: 5 -> 5, of which waited for: 5 -> 5; matrix products, arithmetic and copies ran while one was open for 8% -> 10% of each run, Pallas kernels for 4% -> 4%
where the time goes in v3:
time: 52.3 us; the launch traced here: 51.7 us
  Pallas kernels  15.3 us (29%)
  blocking collectives  12 us (23%)
  starting transfers between devices  11.2 us (21%)
  local copies, waits for them, and re-layouts  7.89 us (15%)
  waiting for transfers between devices  3.98 us (8%)
  between operations  1.38 us (3%)
    pallas_call x6, Pallas kernels, call(): pl.pallas_call(kernel, out_shape=[out if hasattr(out, 'dtype') else jax.S...  15.3 us
    all_to_all x1, blocking collectives, to_all(): return lax.all_to_all(copies, ('gx', 'gy'), 0, 0, tiled=True)  12 us
    all_to_all x1, starting transfers between devices, to_all(): return lax.all_to_all(copies, ('gx', 'gy'), 0, 0, tiled=True)  7.3 us
    unnamed x12, local copies, waits for them, and re-layouts  5.71 us
    ppermute x1, waiting for transfers between devices, exchange(): up = lax.ppermute(up, axes, layout.shift(step, 0))  1.86 us
    ppermute x1, starting transfers between devices, exchange(): before = lax.ppermute(to_before, axes, layout.shift(0, step))  1.78 us
    squeeze x1, local copies, waits for them, and re-layouts, local(): weights = [latent_turned[0], jnp.concatenate(joined, axis=0)]  1.47 us
    ppermute x1, starting transfers between devices, exchange(): down = lax.ppermute(down, axes, layout.shift(-step, 0))  1.11 us
  transfers between devices with their start and end apart: 5, of which 5 were waited for; matrix products, arithmetic and copies ran while one was open for 10% of the time, Pallas kernels for 4%

profile of v3, /device:TPU:0, one launch (start us, length us, event | category | flops | bytes accessed | tf_op | source)
XLA Modules:
  0.0 51.7 jit_solution(13744434458754368604)
XLA Ops:
  1.3 1.6 %shard_map.131 = f32[32,8,128]{2,1,0:T(8,128)} custom-call(s32[1,1]{1,0:T(1,128)} %bitcast.17.refs_0_, f32[3,32]{1,0:T(4,128)} %refs_1_.1, s32[1,32]{1,0:T(1,128)} %bitcast.23, s32[4,8]{1,0:T(4,128)} %bitcast.21, s32[2,256]{1,0:T(2,128)} %bitcast.22), custom_call_target="tpu_custom_call" | custom-call | tf_op jit(solution)/shard_map/pallas_call | solution.py:660
  2.9 7.3 %all-to-all-start = ((f32[32,8,128]{2,1,0:T(8,128)}), f32[32,8,128]{2,1,0:T(8,128)S(1)}, u32[]{:S(2)}, u32[]{:S(2)}) async-start(f32[32,8,128]{2,1,0:T(8,128)} %shard_map.131), calls=%async_computation | async-start | bytes 262144 | tf_op jit(solution)/shard_map/all_to_all | solution.py:679
  10.2 0.7 %bitcast_dynamic-update-slice_fusion.2 = f32[154,512]{1,0:T(8,128)S(1)} fusion(f32[512,8]{0,1:T(8,128)} %param.19), kind=kLoop, calls=%fused_computation.5 | loop fusion | bytes 32768
  10.9 0.7 %bitcast_dynamic-update-slice_fusion.1 = f32[154,512]{1,0:T(8,128)S(1)} fusion(f32[154,512]{1,0:T(8,128)S(1)} %bitcast_dynamic-update-slice_fusion.2, f32[512,8]{0,1:T(8,128)} %param.17), kind=kLoop, calls=%fused_computation.4 | loop fusion | bytes 32768
  11.6 0.7 %bitcast_dynamic-update-slice_fusion = f32[154,512]{1,0:T(8,128)S(1)} fusion(f32[154,512]{1,0:T(8,128)S(1)} %bitcast_dynamic-update-slice_fusion.1, f32[512,8]{0,1:T(8,128)} %param.18), kind=kLoop, calls=%fused_computation.3 | loop fusion | bytes 32768
  12.3 1.0 %constant_dynamic-update-slice_fusion.1 = f32[154,512]{1,0:T(8,128)S(1)} fusion(f32[154,512]{1,0:T(8,128)S(1)} %bitcast_dynamic-update-slice_fusion, f32[128,512]{1,0:T(8,128)} %bitcast.20), kind=kLoop, calls=%fused_computation.7 | loop fusion | bytes 524288
  13.3 0.7 %constant_dynamic-update-slice_fusion.refs_1_ = f32[154,512]{1,0:T(8,128)S(1)} fusion(f32[154,512]{1,0:T(8,128)S(1)} %constant_dynamic-update-slice_fusion.1, f32[2,512]{1,0:T(2,128)} %param.23), kind=kLoop, calls=%fused_computation.6 | loop fusion | bytes 8192 | tf_op jit(solution)/shard_map/concatenate | solution.py:735
  14.0 1.5 %slice_bitcast_fusion.refs_0_ = f32[704,512]{1,0:T(8,128)S(1)} fusion(f32[2,704,512]{2,1,0:T(8,128)} %bitcast.18), kind=kLoop, calls=%fused_computation | loop fusion | bytes 2883584 | tf_op jit(solution)/shard_map/squeeze | solution.py:735
  15.5 0.0 copy-start
  15.5 0.9 %shard_map.132 = (bf16[2,512,704]{2,1,0:T(8,128)(2,1)S(1)}, bf16[3,128,512]{2,1,0:T(8,128)(2,1)S(1)}) custom-call(f32[704,512]{1,0:T(8,128)S(1)} %slice_bitcast_fusion.refs_0_, f32[154,512]{1,0:T(8,128)S(1)} %constant_dynamic-update-slice_fusion.refs_1_), custom_call_target="tpu_custom_call" | custom-call | tf_op jit(solution)/shard_map/pallas_call | solution.py:660
  16.4 0.0 copy-start.1
  16.4 1.2 %copy-done.1 = bf16[2,512,704]{2,1,0:T(8,128)(2,1)} copy-done((bf16[2,512,704]{2,1,0:T(8,128)(2,1)}, bf16[2,512,704]{2,1,0:T(8,128)(2,1)S(1)}, u32[]{:S(2)}) %copy-start.1) | copy-done | bytes 1441816
  17.5 0.8 %all-to-all-done.gathered_ref = f32[32,8,128]{2,1,0:T(8,128)S(1)} async-done(((f32[32,8,128]{2,1,0:T(8,128)}), f32[32,8,128]{2,1,0:T(8,128)S(1)}, u32[]{:S(2)}, u32[]{:S(2)}) %all-to-all-start) | async-done | bytes 131104 | tf_op jit(solution)/shard_map/all_to_all | solution.py:679
  18.4 0.0 copy-start.2
  18.4 1.4 %copy-done.2 = bf16[2,512,704]{2,1,0:T(8,128)(2,1)S(1)} copy-done((bf16[2,512,704]{2,1,0:T(8,128)(2,1)S(1)}, bf16[2,512,704]{2,1,0:T(8,128)(2,1)}, u32[]{:S(2)}) %copy-start.2) | copy-done | bytes 1441816
  19.8 0.0 copy-start.3
  19.8 8.7 %shard_map.133 = (f32[512,256]{1,0:T(8,128)S(1)}, f32[16,256]{1,0:T(8,128)S(1)}, f32[8,128]{1,0:T(8,128)S(1)}, f32[8,128]{1,0:T(8,128)S(1)}, f32[32,576]{1,0:T(8...) custom-call(f32[32,8,128]{2,1,0:T(8,128)S(1)} %all-to-all-done.gathered_ref, ...), custom_call_target="tpu_custom_call" | custom-call | tf_op jit(solution)/shard_map/pallas_call | solution.py:660
  28.5 1.0 %collective-permute-start = (f32[3,4,576]{2,1,0:T(4,128)S(1)}, f32[3,4,576]{2,1,0:T(4,128)S(1)}, u32[]{:S(2)}, u32[]{:S(2)}) collective-permute-start(f32[3,4,576]{2,1,0:T(4,128)S(1)} %get-tuple-element.26), channel_id=1, source_target_pairs={{0,4},{1,5},{2,6},{3,7},{8,0},{9,1},{10,2},{11,3},{16,8},{17,9},{1... | collective-permute-start | bytes 82952 | tf_op jit(solution)/shard_map/ppermute | solution.py:685
  29.5 1.1 %collective-permute-start.1 = (f32[3,4,576]{2,1,0:T(4,128)S(1)}, f32[3,4,576]{2,1,0:T(4,128)S(1)}, u32[]{:S(2)}, u32[]{:S(2)}) collective-permute-start(f32[3,4,576]{2,1,0:T(4,128)S(1)} %get-tuple-element.28), channel_id=1, source_target_pairs={{0,8},{1,9},{2,10},{3,11},{8,16},{9,17},{10,18},{11,19},{16,24},{1... | collective-permute-start | bytes 82952 | tf_op jit(solution)/shard_map/ppermute | solution.py:686
  30.6 1.9 %collective-permute-done.from_up_ref = f32[3,4,576]{2,1,0:T(4,128)S(1)} collective-permute-done((f32[3,4,576]{2,1,0:T(4,128)S(1)}, f32[3,4,576]{2,1,0:T(4,128)S(1)}, u32[]{:S(2)}, u32[]{:S(2)}) %collective-permute-start) | collective-permute-done | bytes 27680 | tf_op jit(solution)/shard_map/ppermute | solution.py:685
  32.4 0.9 %collective-permute-done.1.from_down_ref = f32[3,4,576]{2,1,0:T(4,128)S(1)} collective-permute-done((f32[3,4,576]{2,1,0:T(4,128)S(1)}, f32[3,4,576]{2,1,0:T(4,128)S(1)}, u32[]{:S(2)}, u32[]{:S(2)}) %collective-permute-start.1) | collective-permute-done | bytes 27680 | tf_op jit(solution)/shard_map/ppermute | solution.py:686
  33.4 0.1 collective-permute-start.3
  33.5 1.8 %collective-permute-start.2 = (f32[3,4,576]{2,1,0:T(4,128)S(1)}, f32[3,4,576]{2,1,0:T(4,128)S(1)}, u32[]{:S(2)}, u32[]{:S(2)}) collective-permute-start(f32[3,4,576]{2,1,0:T(4,128)S(1)} %pad_maximum_fusion), channel_id=1, source_target_pairs={{0,3},{1,0},{2,1},{3,2},{8,11},{9,8},{10,9},{11,10},{16,19},{17,16... | collective-permute-start | bytes 82952 | tf_op jit(solution)/shard_map/ppermute | solution.py:689
  35.2 0.0 copy-done
  35.2 0.0 copy-done.3
  35.2 1.2 %shard_map.134 = (f32[512,256]{1,0:T(8,128)S(1)}, bf16[512,192]{1,0:T(8,128)(2,1)S(1)}, bf16[512,192]{1,0:T(8,128)(2,1)S(1)}, bf16[512,512]{1,0:T(8,128)(2,1)S(1)}, bf16[512,512]{1,0:T(8,128)(2,1)S(1)}) custom-call(f32[512,256]{1,0:T(8,128)S(1)} %get-tuple-element.22.hidden_ref.hidden_in_ref, f32[2,704,512]{2,1,0:T(8,128)S(1)} %bitcast.19, ...), custom_call_target="tpu_custom_call" | custom-call | flops 805306368 | bytes 1048576 | tf_op jit(solution)/shard_map/pallas_call | solution.py:660
  36.5 0.3 collective-permute-done.3.after_ref
  36.7 0.1 collective-permute-done.2.before_ref
  36.8 2.1 %shard_map.135 = f32[32,2,128]{2,1,0:T(2,128)S(1)} custom-call(f32[8,128]{1,0:T(8,128)S(1)} %get-tuple-element.21.static_ref, f32[512,256]{1,0:T(8,128)S(1)} %get-tuple-element.22.hidden_ref.hidden_in_ref, f32[512,256]{1,0:T(8,128)S(1)} %get-tuple-element.23.ahead_ref, f32[16,256]{1,0:T(8,128)S(1)} %get-tuple-element.24.geo_ref, ...), custom_call_target="tpu_custom_call" | custom-call | tf_op jit(solution)/shard_map/pallas_call | solution.py:660
  38.9 12.0 %all_to_all.10.gathered_ref = f32[32,2,128]{2,1,0:T(2,128)S(1)} all-to-all(f32[32,2,128]{2,1,0:T(2,128)S(1)} %shard_map.135), channel_id=1, replica_groups=mesh['gx'=8,'gy'=4] {'gx','gy'}, dimensions={0} | all-to-all | bytes 65536 | tf_op jit(solution)/shard_map/all_to_all | solution.py:679
  50.9 0.8 %shard_map.136 = (f32[1,32]{1,0:T(1,128)}, f32[3,32]{1,0:T(4,128)}) custom-call(f32[32,2,128]{2,1,0:T(2,128)S(1)} %all_to_all.10.gathered_ref, f32[8,128]{1,0:T(8,128)S(1)} %get-tuple-element.33.static_ref), custom_call_target="tpu_custom_call" | custom-call | tf_op jit(solution)/shard_map/pallas_call | solution.py:660
  (5 shorter events, 0.0 us)
Async XLA Ops:
  2.9 15.5 %all-to-all-start = ((f32[32,8,128]{2,1,0:T(8,128)}), f32[32,8,128]{2,1,0:T(8,128)S(1)}, u32[]{:S(2)}, u32[]{:S(2)}) async-start(f32[32,8,128]{2,1,0:T(8,128)} %shard_map.131), calls=%async_computation | async-start | bytes 262144 | tf_op jit(solution)/shard_map/all_to_all | solution.py:679
  15.5 19.8 %copy-start = (f32[2,512,704]{1,2,0:T(8,128)S(1)}, f32[2,512,704]{1,2,0:T(8,128)}, u32[]{:S(2)}) copy-start(f32[2,512,704]{1,2,0:T(8,128)} %param.21) | copy-start | bytes 8650756
  16.4 1.2 %copy-start.1 = (bf16[2,512,704]{2,1,0:T(8,128)(2,1)}, bf16[2,512,704]{2,1,0:T(8,128)(2,1)S(1)}, u32[]{:S(2)}) copy-start(bf16[2,512,704]{2,1,0:T(8,128)(2,1)S(1)} %get-tuple-element.20.halves_ref) | copy-start | bytes 4325380
  18.4 1.4 %copy-start.2 = (bf16[2,512,704]{2,1,0:T(8,128)(2,1)S(1)}, bf16[2,512,704]{2,1,0:T(8,128)(2,1)}, u32[]{:S(2)}) copy-start(bf16[2,512,704]{2,1,0:T(8,128)(2,1)} %copy-done.1) | copy-start | bytes 4325380
  19.8 15.4 %copy-start.3 = (f32[512,512]{1,0:T(8,128)S(1)}, f32[512,512]{1,0:T(8,128)}, u32[]{:S(2)}) copy-start(f32[512,512]{1,0:T(8,128)} %out_hbm_ref.1) | copy-start | bytes 3145732
  28.5 3.9 %collective-permute-start = (f32[3,4,576]{2,1,0:T(4,128)S(1)}, f32[3,4,576]{2,1,0:T(4,128)S(1)}, u32[]{:S(2)}, u32[]{:S(2)}) collective-permute-start(f32[3,4,576]{2,1,0:T(4,128)S(1)} %get-tuple-element.26), channel_id=1, source_target_pairs={{0,4},{1,5},{2,6},{3,7},{8,0},{9,1},{10,2},{11,3},{16,8},{17,9},{1... | collective-permute-start | bytes 82952 | tf_op jit(solution)/shard_map/ppermute | solution.py:685
  29.5 3.9 %collective-permute-start.1 = (f32[3,4,576]{2,1,0:T(4,128)S(1)}, f32[3,4,576]{2,1,0:T(4,128)S(1)}, u32[]{:S(2)}, u32[]{:S(2)}) collective-permute-start(f32[3,4,576]{2,1,0:T(4,128)S(1)} %get-tuple-element.28), channel_id=1, source_target_pairs={{0,8},{1,9},{2,10},{3,11},{8,16},{9,17},{10,18},{11,19},{16,24},{1... | collective-permute-start | bytes 82952 | tf_op jit(solution)/shard_map/ppermute | solution.py:686
  33.4 3.4 %collective-permute-start.3 = (f32[3,4,576]{2,1,0:T(4,128)S(1)}, f32[3,4,576]{2,1,0:T(4,128)S(1)}, u32[]{:S(2)}, u32[]{:S(2)}) collective-permute-start(f32[3,4,576]{2,1,0:T(4,128)S(1)} %pad_maximum_fusion.1), channel_id=1, source_target_pairs={{0,1},{1,2},{2,3},{3,0},{8,9},{9,10},{10,11},{11,8},{16,17},{17,18... | collective-permute-start | bytes 82952 | tf_op jit(solution)/shard_map/ppermute | solution.py:690
  33.5 3.4 %collective-permute-start.2 = (f32[3,4,576]{2,1,0:T(4,128)S(1)}, f32[3,4,576]{2,1,0:T(4,128)S(1)}, u32[]{:S(2)}, u32[]{:S(2)}) collective-permute-start(f32[3,4,576]{2,1,0:T(4,128)S(1)} %pad_maximum_fusion), channel_id=1, source_target_pairs={{0,3},{1,0},{2,1},{3,2},{8,11},{9,8},{10,9},{11,10},{16,19},{17,16... | collective-permute-start | bytes 82952 | tf_op jit(solution)/shard_map/ppermute | solution.py:689
